TPU v7x, 32 devices: a whole 2x2x4 slice. The times are simulated.
32 devices in a mesh: dp: 8 (over z, x), rep: 4 (over y, core).
Axes of the slice: x: 2, y: 2, z: 4, core: 2. Of those that a mesh axis runs over, the one named last changes fastest.
Arguments:
- frames: bfloat16 [32, 3, 64, 2000], P(('dp', 'rep')), may hold values from -6 to 6
- weights: bfloat16 [2, 2000, 2000], replicated, may hold values from -0.125 to 0.125
- norm_gain: float32 [2, 2000], replicated, may hold values from 0.25 to 0.75
- norm_shift: float32 [2, 2000], replicated, may hold values from -0.2 to 0.2
- decays: float32 [2, 2000], replicated, may hold values from 0.85 to 0.99
- lengths: int32 [32], P(('dp', 'rep')), may hold values from 1 to 64, as said below
- cotangent: bfloat16 [32, 3, 64, 2000], P(('dp', 'rep')), may hold values from -6 to 6
Outputs:
- output: bfloat16 [32, 3, 64, 2000], P(('dp', 'rep'))
- grad_frames: bfloat16 [32, 3, 64, 2000], P(('dp', 'rep'))
- grad_weights: float32 [2, 2000, 2000], replicated
- grad_gain: float32 [2, 2000], replicated
- grad_shift: float32 [2, 2000], replicated
- grad_decay: float32 [2, 2000], replicated
Inputs may be any that keep to these rules, and one draw needn't show every extreme that they name: `lengths`: each group's number of valid frames, a prefix of its slots; some group has exactly 64.
All inputs are finite; a program needn't handle non-finite values.
Results may differ from a plain program's by a relative error of at most 0.0046.
Values sent between devices are 32-bit elements; how exact they have to be, the bound alone decides.
A program may use at most 256 MiB of HBM per device.

v0:
```python
import jax
import jax.numpy as jnp
from jax import lax
from jax.sharding import PartitionSpec as P

eps = 1e-05


def combine(earlier, latter):
    return (earlier[0] * latter[0], latter[0] * earlier[1] + latter[1])


def recurrence(values, decay_rate, layout, reverse):
    shaped = values.reshape(layout + (values.shape[-1],))
    factors = jnp.broadcast_to(decay_rate, shaped.shape)
    result = lax.associative_scan(combine, (factors, shaped), reverse=reverse, axis=2)
    return result[1].reshape(values.shape)


def first_moments(projected, valid):
    partial_value = (
        jnp.sum(valid * projected, axis=0),
        jnp.sum(valid * projected * projected, axis=0),
        jnp.sum(valid).reshape(1),
    )
    return lax.psum((partial_value[0], partial_value[1], partial_value[2]), ("dp", "rep"))


def later_moments(projected, valid):
    partial_value = (
        jnp.sum(valid * projected, axis=0),
        jnp.sum(valid * projected * projected, axis=0),
        jnp.sum(valid).reshape(1),
    )
    return lax.psum((partial_value[0], partial_value[1], partial_value[2]), ("dp", "rep"))


def run_layer(layer_in, rounded, weight, gain_row, shift_row, decay_rate, valid, layout, moments):
    projected = jnp.dot(rounded, weight, preferred_element_type=jnp.float32)
    first_sum, square_sum, total = moments(projected, valid)
    average = first_sum / total
    variance = square_sum / total - average * average
    inverse_std = lax.rsqrt(variance + eps)
    normed = (projected - average) * inverse_std
    states = recurrence(gain_row * normed + shift_row, decay_rate, layout, False)
    result = layer_in + valid * jax.nn.softplus(states)
    return (result, (normed, inverse_std, states, total))


def back_layer(grad_out, weight, gain_row, decay_rate, valid, layout, saved):
    normed, inverse_std, states, total = saved
    grad_states = valid * grad_out * jax.nn.sigmoid(states)
    carried = recurrence(grad_states, decay_rate, layout, True)
    shaped = states.reshape(layout + (states.shape[-1],))
    previous = jnp.pad(shaped[:, :, :-1], ((0, 0), (0, 0), (1, 0), (0, 0))).reshape(states.shape)
    grad_gain, grad_shift, grad_decay = lax.psum(
        (
            jnp.sum(carried * normed, axis=0),
            jnp.sum(carried, axis=0),
            jnp.sum(carried * previous, axis=0),
        ),
        ("dp", "rep"),
    )
    grad_proj = inverse_std * (
        gain_row * carried - valid * gain_row * (grad_shift + normed * grad_gain) / total
    )
    rounded_grad = grad_proj.astype(jnp.bfloat16)
    backward = lax.dot_general(
        rounded_grad, weight, (((1,), (1,)), ((), ())), preferred_element_type=jnp.float32
    )
    return (grad_out + backward, rounded_grad, grad_gain, grad_shift, grad_decay)


def weight_rows(rounded, rounded_grad):
    return lax.dot_general(
        rounded, rounded_grad, (((0,), (0,)), ((), ())), preferred_element_type=jnp.float32
    )


def body(frames, weights, norm_gain, norm_shift, decays, lengths, cotangent):
    groups = frames.shape[0]
    frame_slots = frames.shape[2]
    hidden = frames.shape[3]
    layout = (groups, frames.shape[1], frame_slots)
    positions = jnp.arange(frame_slots, dtype=jnp.int32)
    valid = jnp.broadcast_to(positions[None, None, :] < lengths[:, None, None], layout)
    valid = valid.reshape(-1, 1).astype(jnp.float32)
    first_in = frames.reshape(-1, hidden)
    middle, saved_one = run_layer(
        first_in.astype(jnp.float32),
        first_in,
        weights[0],
        norm_gain[0],
        norm_shift[0],
        decays[0],
        valid,
        layout,
        first_moments,
    )
    second_in = middle.astype(jnp.bfloat16)
    result, saved_two = run_layer(
        middle,
        second_in,
        weights[1],
        norm_gain[1],
        norm_shift[1],
        decays[1],
        valid,
        layout,
        first_moments,
    )
    middle_again, saved_one = run_layer(
        first_in.astype(jnp.float32),
        first_in,
        weights[0],
        norm_gain[0],
        norm_shift[0],
        decays[0],
        valid,
        layout,
        later_moments,
    )
    second_in = middle_again.astype(jnp.bfloat16)
    result_again, saved_two = run_layer(
        middle_again,
        second_in,
        weights[1],
        norm_gain[1],
        norm_shift[1],
        decays[1],
        valid,
        layout,
        later_moments,
    )
    grad_top = cotangent.reshape(-1, hidden).astype(jnp.float32)
    grad_mid, round_two, gain_two, shift_two, decay_two = back_layer(
        grad_top, weights[1], norm_gain[1], decays[1], valid, layout, saved_two
    )
    grad_first, round_one, gain_one, shift_one, decay_one = back_layer(
        grad_mid, weights[0], norm_gain[0], decays[0], valid, layout, saved_one
    )
    portion = lax.psum_scatter(
        jnp.concatenate(
            [weight_rows(first_in, round_one), weight_rows(second_in, round_two)], axis=1
        ),
        "rep",
        scatter_dimension=0,
        tiled=True,
    )
    flat_portion = portion.reshape(-1)
    summed = lax.psum_scatter(flat_portion, "dp", scatter_dimension=0, tiled=True)
    summed = lax.all_gather(summed, "dp", axis=0, tiled=True).reshape(portion.shape)
    gathered = lax.all_gather(summed, "rep", axis=0, tiled=True)
    grad_weights = jnp.stack([gathered[:, :hidden], gathered[:, hidden:]])
    return (
        result.reshape(frames.shape).astype(jnp.bfloat16),
        grad_first.reshape(frames.shape).astype(jnp.bfloat16),
        grad_weights,
        jnp.stack([gain_one, gain_two]),
        jnp.stack([shift_one, shift_two]),
        jnp.stack([decay_one, decay_two]),
    )


def solution(mesh):
    placed = (
        P(("dp", "rep"), None, None, None),
        P(),
        P(),
        P(),
        P(),
        P(("dp", "rep")),
        P(("dp", "rep"), None, None, None),
    )
    return jax.shard_map(
        body,
        mesh=mesh,
        in_specs=placed,
        out_specs=(
            P(("dp", "rep"), None, None, None),
            P(("dp", "rep"), None, None, None),
            P(),
            P(),
            P(),
            P(),
        ),
        check_vma=False,
    )
```

profile of v0, /device:TPU:31, one launch (start us, length us, event | category | flops | bytes accessed | tf_op | source)
XLA Modules:
  0.0 2027.5 jit_solution(7453121888070470627)
XLA Ops:
  11.4 5.5 multiply_reduce_fusion.1
  16.9 38.7 %all-reduce.56 = (f32[2000]{0:T(1024)S(1)}, f32[]{:T(128)}, f32[2000]{0:T(1024)S(1)}) all-reduce(f32[2000]{0:T(1024)S(1)} %get-tuple-element.9, f32[]{:T(128)} %broadcast_reduce_fusion, f32[2000]{0:T(1024)S(1)} %get-tuple-element.8), channel_id=1, replica_groups=mesh['dp'=8,'rep'=4] {'dp','rep'}, use_global_device_ids=true, to_apply=%region_5.0 | all-reduce | flops 4001 | bytes 32008 | tf_op jit(solution)/shard_map/psum | solution.py:26
  112.3 4.1 pad.189
  116.4 3.8 fusion.73
  120.2 5.3 multiply_reduce_fusion
  125.5 40.6 %all-reduce.55 = (f32[2000]{0:T(1024)S(1)}, f32[2000]{0:T(1024)S(1)}) all-reduce(f32[2000]{0:T(1024)S(1)} %get-tuple-element.7, f32[2000]{0:T(1024)S(1)} %get-tuple-element.6), channel_id=1, replica_groups=mesh['dp'=8,'rep'=4] {'dp','rep'}, use_global_device_ids=true, to_apply=%region_9.10 | all-reduce | flops 4000 | bytes 32000 | tf_op jit(solution)/shard_map/psum | solution.py:26
  168.3 4.5 slice.725
  225.4 4.3 pad.201
  232.7 3.7 divide_multiply_fusion
  236.4 4.5 slice.763
  243.1 8.6 slice.764
  251.6 8.6 slice.766
  261.1 8.6 slice.762
  336.4 4.3 pad.214
  340.6 8.6 slice.804
  350.2 8.7 slice.761
  361.5 4.2 pad.213
  368.4 7.5 rev.4
  378.2 40.3 %all-reduce.54 = (f32[2000]{0:T(1024)S(1)}, f32[2000]{0:T(1024)S(1)}) all-reduce(f32[2000]{0:T(1024)S(1)} %fusion.46, f32[2000]{0:T(1024)S(1)} %get-tuple-element.13), channel_id=1, replica_groups=mesh['dp'=8,'rep'=4] {'dp','rep'}, use_global_device_ids=true, to_apply=%region_13.14 | all-reduce | flops 4000 | bytes 32000 | tf_op jit(solution)/shard_map/psum | solution.py:56
  421.5 8.5 fusion.30
  434.5 8.6 slice.809
  443.1 8.6 slice.811
  451.8 5.2 slice.807
  483.7 4.4 slice.848
  500.1 4.2 pad.226
  504.3 8.6 slice.849
  513.8 8.7 slice.806
  525.1 4.1 pad.225
  532.0 7.6 rev.5
  542.3 8.4 fusion.92
  550.7 40.6 %all-reduce.53 = (f32[2000]{0:T(1024)S(1)}, f32[2000]{0:T(1024)S(1)}, f32[1,2000]{1,0:T(1,128)S(1)}, f32[1,2000]{1,0:T(1,128)S(1)}) all-reduce(f32[2000]{0:T(1024)S(1)} %fusion.34, f32[2000]{0:T(1024)S(1)} %get-tuple-element.11, f32[1,2000]{1,0:T(1,128)S(1)} %bitcast.141, ...), channel_id=1, replica_groups=mesh['dp'=8,'rep'=4] {'dp','rep'}, use_global_device_ids=true, to_apply=%region_17.18 | all-reduce | flops 8000 | bytes 64000 | tf_op jit(solution)/shard_map/psum | solution.py:56
  595.9 3.3 copy-done
  599.2 11.5 pad_maximum_fusion
  612.6 545.5 %all-reduce.63.cloned.1.call-done = f32[2000,4000]{0,1:T(8,128)} async-done(((f32[2000,4000]{0,1:T(8,128)}), f32[2000,4000]{0,1:T(8,128)}) %all-reduce.63.cloned.1.call-update) | async-done | bytes 32000016
  1158.1 9.3 constant_dynamic-slice_fusion
  1167.4 8.8 copy.17
  1176.2 9.9 reshape.142
  1188.6 256.0 %all-reduce.65.cloned.1.call-done = f32[2000000]{0:T(1024)} async-done(((f32[2000000]{0:T(1024)}), f32[2000000]{0:T(1024)}) %all-reduce.65.cloned.1.call-update) | async-done | bytes 8000016
  1444.7 3.5 broadcast.197
  1451.5 259.0 %all-reduce.61.cloned.1.call-done = f32[2000000]{0:T(1024)} async-done(((f32[2000000]{0:T(1024)}), f32[2000000]{0:T(1024)}) %all-reduce.61.cloned.1.call-update) | async-done | bytes 8000016
  1710.4 9.9 reshape.149
  1720.4 9.0 copy.18
  1731.1 6.9 fusion.18
  1737.9 189.4 %all-gather.3.cloned.1.call-done = f32[4,500,4000]{1,2,0:T(8,128)} async-done(((f32[1,500,4000]{1,2,0:T(8,128)}), f32[4,500,4000]{1,2,0:T(8,128)}) %all-gather.3.cloned.1.call-update) | async-done | bytes 32000016 | tf_op jit(solution)/shard_map/all_gather | solution.py:153
  1927.3 30.6 %copy.19 = f32[4,500,4000]{2,1,0:T(8,128)} copy(f32[4,500,4000]{1,2,0:T(8,128)} %all-gather.3.cloned.1.call-done) | data formatting | bytes 64000000 | tf_op jit(solution)/shard_map/all_gather | solution.py:153
  1957.9 26.8 %reshape.150 = f32[2000,4000]{1,0:T(8,128)} reshape(f32[4,500,4000]{2,1,0:T(8,128)} %copy.19) | data formatting | bytes 64000000
  1984.7 17.2 slice_bitcast_fusion.1
  2001.9 18.6 pad_maximum_fusion.1
  (423 shorter events, 262.5 us)
Async XLA Ops:
  7.2 1151.0 %all-reduce.63.cloned.1.call-start = ((), (), s32[]{:S(2)}) async-start(), calls=%async_computation.2 | async-start | bytes 65536000
  8.6 8.3 copy-start.77
  10.0 46.3 %copy-start.61 = (f32[1,2000]{1,0:T(1,128)}, f32[1,2000]{1,0:T(1,128)S(1)}, u32[]{:S(2)}) copy-start(f32[1,2000]{1,0:T(1,128)S(1)} %get-tuple-element.70) | copy-start | bytes 24004
  56.9 4.3 copy-start.76
  97.3 4.5 copy-start.37
  97.3 4.5 copy-start.69
  108.9 7.5 copy-start.2
  112.2 4.1 copy-start.82
  116.4 3.9 copy-start.78
  120.2 46.6 %copy-start.63 = (f32[1,2000]{1,0:T(1,128)S(1)}, f32[1,2000]{1,0:T(1,128)}, u32[]{:S(2)}) copy-start(f32[1,2000]{1,0:T(1,128)} %get-tuple-element.69) | copy-start | bytes 24004
  120.2 46.6 %copy-start.71 = (f32[1,2000]{1,0:T(1,128)S(1)}, f32[1,2000]{1,0:T(1,128)}, u32[]{:S(2)}) copy-start(f32[1,2000]{1,0:T(1,128)} %get-tuple-element.71) | copy-start | bytes 24004
  125.5 42.7 %copy-start.1 = (f32[192,2000]{1,0:T(8,128)}, f32[192,2000]{1,0:T(8,128)S(1)}, u32[]{:S(2)}) copy-start(f32[192,2000]{1,0:T(8,128)S(1)} %get-tuple-element.88) | copy-start | bytes 4608004
  168.3 4.5 copy-start.5
  211.0 4.5 copy-start.38
  211.0 4.5 copy-start.70
  229.7 2.9 copy-start.18
  229.7 3.1 copy-start.35
  229.7 3.1 copy-start.83
  236.4 4.5 copy-start.6
  328.6 4.6 copy-start.41
  328.6 4.6 copy-start.42
  361.5 4.2 copy-start.16
  368.4 7.5 copy-start.48
  368.4 7.5 copy-start.50
  377.8 40.7 %copy-start.64 = (f32[1,2000]{1,0:T(1,128)S(1)}, f32[1,2000]{1,0:T(1,128)}, u32[]{:S(2)}) copy-start(f32[1,2000]{1,0:T(1,128)} %get-tuple-element.69) | copy-start | bytes 24004
  377.8 40.7 %copy-start.79 = (f32[192]{0:T(256)S(1)}, f32[192]{0:T(256)}, u32[]{:S(2)}) copy-start(f32[192]{0:T(256)} %copy-done.77) | copy-start | bytes 2308
  418.5 3.0 copy-start.72
  418.5 3.0 copy-start.74
  418.5 3.0 copy-start.8
  418.5 3.0 copy-start.19
  418.5 3.0 copy-start.36
  421.4 8.6 copy-start.23
  430.0 4.5 copy-start.22
  458.7 5.8 copy-start.20
  458.7 5.8 copy-start.21
  469.2 5.2 copy-start.27
  476.6 13.0 copy-start.3
  492.3 4.6 copy-start.39
  492.3 4.6 copy-start.40
  525.1 4.1 copy-start.17
  532.0 7.6 copy-start.44
  532.0 7.6 copy-start.46
  542.3 49.0 %copy-start.62 = (f32[1,2000]{1,0:T(1,128)S(1)}, f32[1,2000]{1,0:T(1,128)}, u32[]{:S(2)}) copy-start(f32[1,2000]{1,0:T(1,128)} %copy-done.61) | copy-start | bytes 24004
  542.3 49.0 %copy-start.80 = (f32[192]{0:T(256)S(1)}, f32[192]{0:T(256)}, u32[]{:S(2)}) copy-start(f32[192]{0:T(256)} %copy-done.77) | copy-start | bytes 2308
  593.6 5.7 copy-start
  610.8 833.9 %all-reduce.65.cloned.1.call-start = ((), (), s32[]{:S(2)}) async-start(), calls=%async_computation.3 | async-start | bytes 16007168
  1186.1 524.3 %all-reduce.61.cloned.1.call-start = ((), (), s32[]{:S(2)}) async-start(), calls=%async_computation | async-start | bytes 16007168
  1451.4 475.9 %all-gather.3.cloned.1.call-start = ((), (), s32[]{:S(2)}) async-start(), calls=%async_computation.1 | async-start | bytes 40960000 | tf_op jit(solution)/shard_map/all_gather | solution.py:153
  (43 other events, 53.2 us)
Sparse Core Ops, SparseCore 0:
  610.9 547.2 all-reduce.62
  1186.2 258.3 all-reduce.64
  1451.5 258.8 all-reduce.60
  1729.5 197.7 all-gather.2
where the time goes:
time: 2050 us; the launch traced here: 2030 us
  waiting for transfers between devices  1250 us (61%)
  local copies, waits for them, and re-layouts  430 us (21%)
  blocking collectives  160 us (8%)
  other arithmetic  132 us (6%)
  matrix products  36.9 us (2%)
    unnamed x7, waiting for transfers between devices  1060 us
    slice x108, local copies, waits for them, and re-layouts, recurrence(): lax.associative_scan(combine, (factors, shaped), reverse=reverse, axis=2)  229 us
    all_gather x1, waiting for transfers between devices, body(): gathered = lax.all_gather(summed, 'rep', axis=0, tiled=True)  189 us
    psum x2, blocking collectives, back_layer(): lax.psum((jnp.sum(carried * normed, axis=0), jnp.sum(carried, axis=0), jn...  80.8 us
    psum x2, blocking collectives, first_moments(): lax.psum((partial_value[0], partial_value[1], partial_value[2]), ('dp', '...  79.3 us
    unnamed x182, local copies, waits for them, and re-layouts  78.6 us
  transfers between devices with their start and end apart: 4, of which 4 were waited for; matrix products, arithmetic and copies ran while one was open for 0% of the time, Pallas kernels for 0%

commit v1 on v0

v1 whole, which is shorter than its diff:
```python
import functools

import jax
import jax.numpy as jnp
from jax import lax
from jax.experimental import pallas as pl
from jax.experimental.pallas import tpu as pltpu
from jax.sharding import PartitionSpec as P

EPS = 1e-05
MESH = pl.DeviceIdType.MESH
F32 = jnp.float32
BF16 = jnp.bfloat16
LANES = 128


def round_up(value, unit):
    return -(-value // unit) * unit


def pick_chunks(hidden, ring):
    best = None
    for chunks in (3, 4, 2, 1):
        shard = round_up(-(-hidden // ring), 8 * chunks)
        if best is None or shard * ring < best[0]:
            best = (shard * ring, chunks, shard // chunks)
    return best


def kernel(
    dims,
    frames,
    weights,
    gain,
    shift,
    decay,
    lengths,
    cotangent,
    output,
    grad_frames,
    grad_weights,
    grad_gain,
    grad_shift,
    grad_decay,
    wbuf,
    x0f,
    x1,
    x1r,
    xb,
    normed,
    states,
    gy,
    gpf,
    gpb,
    xr,
    gr,
    xchunk,
    gb,
    dw,
    ro,
    ra,
    params,
    coef,
    eight_f,
    eight_b,
    ring_f,
    ring_b,
    total_f,
    total_b,
    sem_w,
    sem_x,
    sem_g,
    sem_e,
    sem_r,
    sem_ro,
    sem_ra,
    sem_aa,
    sem_ag,
    sem_l,
):
    ring, chunks, chunk_rows, views, slots, hidden, width = dims
    rows = views * slots
    quarter = width // 4
    half = quarter // 2
    padded = ring * chunks * chunk_rows
    blocks = slots // 8
    lane_steps = width // LANES

    dp, rep = lax.axis_index("dp"), lax.axis_index("rep")
    a, bx = dp // 2, dp % 2
    by, c = rep // 2, rep % 2
    nx, ny, nc = 1 - bx, 1 - by, 1 - c

    def device(a_at, x_at, y_at, c_at):
        return (a_at * 2 + x_at, y_at * 2 + c_at)

    core_peer = device(a, bx, by, nc)
    x_peer = device(a, nx, by, c)
    y_peer = device(a, bx, ny, c)

    def group_peer(flips):
        fx, fy, fc = flips // 4, flips // 2 % 2, flips % 2
        x_at, y_at, c_at = (nx if fx else bx), (ny if fy else by), (nc if fc else c)
        return device(a, x_at, y_at, c_at), x_at * 4 + y_at * 2 + c_at

    def ring_peer(step):
        a_at = lax.rem(a + step, ring)
        return device(a_at, bx, by, c), a_at

    def each_ring(act):
        if ring <= 8:
            for step in range(1, ring):
                act(step)
        else:

            def go(step, _):
                act(step)
                return 0

            lax.fori_loop(1, ring, go, 0)

    def remote(src, dst, sems, at, target):
        return pltpu.make_async_remote_copy(
            src_ref=src,
            dst_ref=dst,
            send_sem=sems.at[(0,) + at],
            recv_sem=sems.at[(1,) + at],
            device_id=target,
            device_id_type=MESH,
        )

    barrier = pltpu.get_barrier_semaphore()
    for flips in range(1, 8):
        pl.semaphore_signal(barrier, 1, device_id=group_peer(flips)[0], device_id_type=MESH)
    each_ring(
        lambda step: pl.semaphore_signal(
            barrier, 1, device_id=ring_peer(step)[0], device_id_type=MESH
        )
    )

    def load_weight(layer, at):
        return pltpu.make_async_copy(weights.at[layer], wbuf, sem_w.at[at])

    load_weight(0, 0).start()

    x0f[:, pl.ds(hidden - hidden % LANES, width - hidden + hidden % LANES)] = jnp.zeros(
        (rows, width - hidden + hidden % LANES), F32
    )
    x0f[:, :hidden] = frames[...].astype(F32)
    params[...] = jnp.zeros(params.shape, F32)
    for at, source in enumerate((gain, shift, decay)):
        params[at * 2 : at * 2 + 2, :hidden] = source[...]
    pl.semaphore_wait(barrier, 7 + ring - 1)

    pair_peer = (x_peer, y_peer)
    other_peer = (y_peer, x_peer)
    pair_at = (bx, by)
    other_at = (by, bx)
    far_pair = (nx, ny)
    diagonal = (device(a, nx, by, nc), device(a, bx, ny, nc))
    sent_x = (x0f, x1r)

    def send_x(layer):
        to_pair = remote(sent_x[layer], xr.at[layer, 0], sem_x, (layer, 0), pair_peer[layer])
        to_core = remote(sent_x[layer], xr.at[layer, 1], sem_x, (layer, 1), core_peer)
        to_pair.start()
        to_core.start()

    def forward_x(layer):
        remote(sent_x[layer], xr.at[layer, 0], sem_x, (layer, 0), pair_peer[layer]).wait_recv()
        remote(xr.at[layer, 0], xr.at[layer, 2], sem_x, (layer, 2), core_peer).start()

    send_x(0)

    row_at = lax.broadcasted_iota(jnp.int32, (8, LANES), 0)
    length = lengths[0]

    def lanes_of(step):
        return pl.ds(pl.multiple_of(step * LANES, LANES), LANES)

    def over_lanes(act):
        def go(step, _):
            act(lanes_of(step), step)
            return 0

        lax.fori_loop(0, lane_steps, go, 0)

    def valid_at(block):
        return (row_at + block * 8) < length

    def spread(row):
        return jnp.broadcast_to(row, (8, LANES))

    def row_powers(decay_row, reverse):
        one = spread(decay_row)
        two = one * one
        four = two * two
        from_edge = 7 - row_at if reverse else row_at
        ones = jnp.ones((8, LANES), F32)
        power = (
            one
            * jnp.where(from_edge % 2 == 1, one, ones)
            * jnp.where(from_edge // 2 % 2 == 1, two, ones)
            * jnp.where(from_edge // 4 == 1, four, ones)
        )
        zero = jnp.zeros((8, LANES), F32)
        return (
            jnp.where(from_edge >= 1, one, zero),
            jnp.where(from_edge >= 2, two, zero),
            jnp.where(from_edge >= 4, four, zero),
            power,
        )

    def scan_blocks(values, powers, reverse):
        one, two, four, power = powers
        count = len(values)
        order = range(count - 1, -1, -1) if reverse else range(count)
        result = [None] * count
        carry = None
        for at in order:
            value = values[at]
            for amount, factor in ((1, one), (2, two), (4, four)):
                value = value + factor * pltpu.roll(value, 8 - amount if reverse else amount, 0)
            if carry is not None:
                value = value + power * carry
            carry = spread(value[0:1] if reverse else value[7:8])
            result[at] = value
        return result

    def project(layer, source):
        for at in range(0, hidden, quarter):
            span = min(quarter, hidden - at)
            normed[layer, :, at : at + span] = jnp.dot(
                source[:, :hidden], wbuf[:, at : at + span], preferred_element_type=F32
            )
        tail = hidden - hidden % LANES
        if tail < hidden:
            kept = normed[layer, :, tail:width]
            lane = lax.broadcasted_iota(jnp.int32, kept.shape, 1)
            normed[layer, :, tail:width] = jnp.where(lane < hidden - tail, kept, 0.0)

    mine = bx * 4 + by * 2 + c

    def moments(layer):
        frame_count = (views * length).astype(F32)

        def act(lanes, step):
            first = jnp.zeros((8, LANES), F32)
            square = jnp.zeros((8, LANES), F32)
            for view in range(views):
                for block in range(blocks):
                    value = normed[layer, view * slots + block * 8 : view * slots + block * 8 + 8, lanes]
                    value = jnp.where(valid_at(block), value, 0.0)
                    first += value
                    square += value * value
            first = jnp.sum(first, axis=0, keepdims=True)
            lane = lax.broadcasted_iota(jnp.int32, (1, LANES), 1) + step * LANES
            first = jnp.where(lane >= hidden, frame_count, first)
            eight_f[layer, mine, 0:1, lanes] = first
            eight_f[layer, mine, 1:2, lanes] = jnp.sum(square, axis=0, keepdims=True)

        over_lanes(act)

    def start_sum(eight, at):
        for flips in range(1, 8):
            peer, _ = group_peer(flips)
            remote(eight.at[mine], eight.at[mine], sem_e, (at, flips - 1), peer).start()

    def middle_sum(eight, around, at):
        for flips in range(1, 8):
            peer, slot = group_peer(flips)
            remote(eight.at[mine], eight.at[slot], sem_e, (at, flips - 1), peer).wait_recv()
        total = eight[0]
        for slot in range(1, 8):
            total = total + eight[slot]
        around[a] = total

        def send(step):
            peer, _ = ring_peer(step)
            remote(around.at[a], around.at[a], sem_r, (at, step), peer).start()

        each_ring(send)

    def finish_sum(eight, around, at, result):
        def wait(step):
            behind = lax.rem(a + ring - step, ring)
            remote(
                around.at[a], around.at[behind], sem_r, (at, step), device(behind, bx, by, c)
            ).wait_recv()

        each_ring(wait)
        total = around[0]
        for slot in range(1, ring):
            total = total + around[slot]
        result[...] = total

    def statistics(layer, lanes):
        count = jnp.broadcast_to(total_f[layer, 0:1, width - 1 : width], (1, LANES))
        average = total_f[layer, 0:1, lanes] / count
        variance = total_f[layer, 1:2, lanes] / count - average * average
        return average, lax.rsqrt(variance + EPS), count

    def forward(layer):
        def act(lanes, step):
            average, inverse, _ = statistics(layer, lanes)
            coef[layer : layer + 1, lanes] = inverse
            average, inverse = spread(average), spread(inverse)
            gain_row = spread(params[layer : layer + 1, lanes])
            shift_row = spread(params[2 + layer : 3 + layer, lanes])
            powers = row_powers(params[4 + layer : 5 + layer, lanes], False)
            for view in range(views):
                drives = []
                for block in range(blocks):
                    at = view * slots + block * 8
                    value = (normed[layer, at : at + 8, lanes] - average) * inverse
                    normed[layer, at : at + 8, lanes] = value
                    drives.append(gain_row * value + shift_row)
                result = scan_blocks(drives, powers, False)
                for block in range(blocks):
                    at = view * slots + block * 8
                    state = result[block]
                    states[layer, at : at + 8, lanes] = state
                    bump = jnp.maximum(state, 0.0) + jnp.log1p(jnp.exp(-jnp.abs(state)))
                    bump = jnp.where(valid_at(block), bump, 0.0)
                    if layer == 0:
                        following = x0f[at : at + 8, lanes] + bump
                        x1[at : at + 8, lanes] = following
                        x1r[at : at + 8, lanes] = following.astype(BF16).astype(F32)
                    else:
                        x1[at : at + 8, lanes] = x1[at : at + 8, lanes] + bump

        over_lanes(act)

    def backward_sums(layer):
        def act(lanes, step):
            powers = row_powers(params[4 + layer : 5 + layer, lanes], True)
            sums = [jnp.zeros((8, LANES), F32) for _ in range(3)]
            for view in range(views):
                sources = []
                kept = []
                for block in range(blocks):
                    at = view * slots + block * 8
                    state = states[layer, at : at + 8, lanes]
                    kept.append(state)
                    slope = 1.0 / (1.0 + jnp.exp(-state))
                    slope = gy[at : at + 8, lanes] * slope
                    sources.append(jnp.where(valid_at(block), slope, 0.0))
                carried = scan_blocks(sources, powers, True)
                for block in range(blocks):
                    at = view * slots + block * 8
                    value = carried[block]
                    gpf[layer, at : at + 8, lanes] = value
                    shifted = pltpu.roll(kept[block], 1, 0)
                    before = spread(kept[block - 1][7:8]) if block else jnp.zeros((8, LANES), F32)
                    shifted = jnp.where(row_at == 0, before, shifted)
                    sums[0] += value * normed[layer, at : at + 8, lanes]
                    sums[1] += value
                    sums[2] += value * shifted
            for at in range(3):
                eight_b[layer, mine, at : at + 1, lanes] = jnp.sum(sums[at], axis=0, keepdims=True)
            eight_b[layer, mine, 3:4, lanes] = jnp.zeros((1, LANES), F32)

        over_lanes(act)

    def backward_drive(layer):
        grad_gain[layer : layer + 1, :] = total_b[layer, 0:1, :hidden]
        grad_shift[layer : layer + 1, :] = total_b[layer, 1:2, :hidden]
        grad_decay[layer : layer + 1, :] = total_b[layer, 2:3, :hidden]

        def act(lanes, step):
            count = jnp.broadcast_to(total_f[layer, 0:1, width - 1 : width], (1, LANES))
            slope = spread(total_b[layer, 0:1, lanes] / count)
            offset = spread(total_b[layer, 1:2, lanes] / count)
            scale = spread(coef[layer : layer + 1, lanes] * params[layer : layer + 1, lanes])
            for view in range(views):
                for block in range(0, blocks, 2):
                    pair = []
                    for side in range(2):
                        at = view * slots + (block + side) * 8
                        drop = offset + normed[layer, at : at + 8, lanes] * slope
                        drop = jnp.where(valid_at(block + side), drop, 0.0)
                        pair.append(scale * (gpf[layer, at : at + 8, lanes] - drop))
                    at = view * slots + block * 8
                    low = jnp.concatenate(pair, axis=0).astype(BF16)
                    gpb[at : at + 16, lanes] = low
                    gpf[layer, at : at + 16, lanes] = low.astype(F32)

        over_lanes(act)

    def quarter_at(p_at, c_at):
        return pl.ds(pl.multiple_of((p_at * 2 + c_at) * quarter, quarter), quarter)

    def grad_copies(layer):
        own, far = pair_at[layer], far_pair[layer]
        return [
            remote(gpf.at[layer, :, quarter_at(p_at, c_at)], gr.at[layer, at], sem_g, (layer, at), peer)
            for at, (p_at, c_at, peer) in enumerate(
                ((far, c, pair_peer[layer]), (own, nc, core_peer), (far, nc, diagonal[layer]))
            )
        ]

    def back_project():
        for at in range(0, hidden, quarter):
            span = min(quarter, hidden - at)
            gy[:, at : at + span] += lax.dot_general(
                gpb[:, :hidden],
                wbuf[at : at + span, :],
                (((1,), (1,)), ((), ())),
                preferred_element_type=F32,
            )

    def wait_factors(layer):
        remote(sent_x[layer], xr.at[layer, 1], sem_x, (layer, 1), core_peer).wait_recv()
        remote(xr.at[layer, 0], xr.at[layer, 2], sem_x, (layer, 2), core_peer).wait_recv()
        for copy in grad_copies(layer):
            copy.wait_recv()

    def weight_product(layer):
        gb[0:rows, :] = gpf[layer, :, quarter_at(pair_at[layer], c)].astype(BF16)
        for at in range(3):
            gb[(at + 1) * rows : (at + 2) * rows, :] = gr[layer, at].astype(BF16)
        for start in range(0, width, quarter):
            span = min(quarter, padded - start)
            xchunk[0:rows, :] = sent_x[layer][:, start : start + quarter].astype(BF16)
            for at in range(3):
                xchunk[(at + 1) * rows : (at + 2) * rows, :] = xr[
                    layer, at, :, start : start + quarter
                ].astype(BF16)
            product = lax.dot_general(
                xchunk[...], gb[...], (((0,), (0,)), ((), ())), preferred_element_type=F32
            )
            dw[layer, start : start + span, :] = product[:span]
        if padded > width:
            dw[layer, width:padded, :] = jnp.zeros((padded - width, quarter), F32)

    def half_at(o_at):
        return pl.ds(pl.multiple_of(o_at * half, half), half)

    def dw_parts(layer):
        return dw.at[layer].reshape(ring, chunks, chunk_rows, quarter)

    def copy_half(layer, k):
        return remote(
            dw_parts(layer).at[:, k, :, half_at(1 - other_at[layer])],
            ro.at[layer, :, k],
            sem_ro,
            (layer, k),
            other_peer[layer],
        )

    def reduce_half(layer, k):
        copy_half(layer, k).wait_recv()
        for at in range(ring):
            start = (at * chunks + k) * chunk_rows
            ro[layer, at, k] = (
                ro[layer, at, k] + dw[layer, start : start + chunk_rows, half_at(other_at[layer])]
            )

        def send(step):
            peer, a_at = ring_peer(step)
            remote(
                ro.at[layer, a_at, k], ra.at[layer, a, k], sem_ra, (layer, k, step), peer
            ).start()

        each_ring(send)

    def column(layer, p_at, o_at, c_at):
        return pl.ds(pl.multiple_of((p_at * 2 + c_at) * quarter + o_at * half, half), half)

    def own_column(layer):
        return column(layer, pair_at[layer], other_at[layer], c)

    def reduce_ring(layer, k):
        def wait(step):
            behind = lax.rem(a + ring - step, ring)
            remote(
                ro.at[layer, a, k],
                ra.at[layer, behind, k],
                sem_ra,
                (layer, k, step),
                device(behind, bx, by, c),
            ).wait_recv()

        each_ring(wait)

        def add(step, total):
            return total + ra[layer, lax.rem(a + step, ring), k]

        total = ro[layer, a, k]
        if ring <= 8:
            for step in range(1, ring):
                total = add(step, total)
        else:
            total = lax.fori_loop(1, ring, add, total)
        ro[layer, a, k] = total
        local_copy(layer, k).start()

        def send(step):
            peer, _ = ring_peer(step)
            remote(
                ro.at[layer, a, k],
                grad_weights.at[layer, a, k, :, own_column(layer)],
                sem_aa,
                (layer, k, step),
                peer,
            ).start()

        each_ring(send)

    def local_copy(layer, k):
        return pltpu.make_async_copy(
            ro.at[layer, a, k],
            grad_weights.at[layer, a, k, :, own_column(layer)],
            sem_l.at[layer, k],
        )

    def gathered(layer, k, p_at, o_at, c_at):
        return grad_weights.at[layer, :, k, :, column(layer, p_at, o_at, c_at)]

    def order_of(layer, k):
        pair_first = (k + layer) % 2 == 1
        own = (pair_at[layer], other_at[layer])
        flip_p = (far_pair[layer], other_at[layer])
        flip_o = (pair_at[layer], 1 - other_at[layer])
        both = (far_pair[layer], 1 - other_at[layer])
        if pair_first:
            return (own, flip_p, flip_o, both), pair_peer[layer], other_peer[layer]
        return (own, flip_o, flip_p, both), other_peer[layer], pair_peer[layer]

    def block_copy(layer, k, kind):
        spots, first, second = order_of(layer, k)
        spot, peer = {
            0: (0, first),
            1: (0, second),
            2: (1, second),
            3: (0, core_peer),
            4: (1, core_peer),
            5: (2, core_peer),
            6: (3, core_peer),
        }[kind]
        region = gathered(layer, k, *spots[spot], c)
        return remote(region, region, sem_ag, (layer, k, kind), peer)

    def arrived(layer, k, kind):
        spots, first, second = order_of(layer, k)
        spot = {0: 1, 1: 2, 2: 3, 3: 0, 4: 1, 5: 2, 6: 3}[kind]
        region = gathered(layer, k, *spots[spot], nc if kind >= 3 else c)
        remote(region, region, sem_ag, (layer, k, kind), core_peer).wait_recv()

    def gather_ring(layer, k):
        def wait(step):
            behind = lax.rem(a + ring - step, ring)
            remote(
                ro.at[layer, a, k],
                grad_weights.at[layer, behind, k, :, own_column(layer)],
                sem_aa,
                (layer, k, step),
                device(behind, bx, by, c),
            ).wait_recv()

        each_ring(wait)
        local_copy(layer, k).wait()
        block_copy(layer, k, 0).start()
        block_copy(layer, k, 1).start()
        block_copy(layer, k, 3).start()

    def gather_first(layer, k):
        arrived(layer, k, 0)
        block_copy(layer, k, 2).start()
        block_copy(layer, k, 4).start()

    def gather_second(layer, k):
        arrived(layer, k, 1)
        block_copy(layer, k, 5).start()
        arrived(layer, k, 2)
        block_copy(layer, k, 6).start()

    xb[...] = x0f[...].astype(BF16)
    load_weight(0, 0).wait()
    project(0, xb)
    load_weight(1, 1).start()
    moments(0)
    start_sum(eight_f.at[0], 0)
    gy[:, pl.ds(hidden - hidden % LANES, width - hidden + hidden % LANES)] = jnp.zeros(
        (rows, width - hidden + hidden % LANES), F32
    )
    gy[:, :hidden] = cotangent[...].astype(F32)
    middle_sum(eight_f.at[0], ring_f.at[0], 0)
    finish_sum(eight_f.at[0], ring_f.at[0], 0, total_f.at[0])
    forward(0)
    send_x(1)
    xb[...] = x1r[...].astype(BF16)
    load_weight(1, 1).wait()
    project(1, xb)
    moments(1)
    start_sum(eight_f.at[1], 1)
    middle_sum(eight_f.at[1], ring_f.at[1], 1)
    finish_sum(eight_f.at[1], ring_f.at[1], 1, total_f.at[1])
    forward(1)
    backward_sums(1)
    start_sum(eight_b.at[1], 2)
    output[...] = x1[:, :hidden].astype(BF16)
    middle_sum(eight_b.at[1], ring_b.at[1], 2)
    finish_sum(eight_b.at[1], ring_b.at[1], 2, total_b.at[1])
    backward_drive(1)
    for copy in grad_copies(1):
        copy.start()
    back_project()
    load_weight(0, 2).start()
    backward_sums(0)
    start_sum(eight_b.at[0], 3)
    forward_x(0)
    middle_sum(eight_b.at[0], ring_b.at[0], 3)
    finish_sum(eight_b.at[0], ring_b.at[0], 3, total_b.at[0])
    backward_drive(0)
    for copy in grad_copies(0):
        copy.start()
    forward_x(1)
    wait_factors(1)
    weight_product(1)
    for k in range(chunks):
        copy_half(1, k).start()
    load_weight(0, 2).wait()
    back_project()
    grad_frames[...] = gy[:, :hidden].astype(BF16)
    wait_factors(0)
    weight_product(0)
    for k in range(chunks):
        copy_half(0, k).start()

    stages = (reduce_half, reduce_ring, gather_ring, gather_first, gather_second)
    tasks = []
    for layer in (1, 0):
        for k in range(chunks):
            for at, stage in enumerate(stages):
                tasks.append(((1 - layer) * chunks + k + at, at, layer, k, stage))
    tasks.sort(key=lambda task: (task[0], -task[1]))
    for _, _, layer, k, stage in tasks:
        stage(layer, k)

    for layer in (1, 0):
        for k in range(chunks):
            for kind in range(3, 7):
                arrived(layer, k, kind)
    for layer in range(2):
        remote(sent_x[layer], xr.at[layer, 0], sem_x, (layer, 0), pair_peer[layer]).wait_send()
        remote(sent_x[layer], xr.at[layer, 1], sem_x, (layer, 1), core_peer).wait_send()
        remote(xr.at[layer, 0], xr.at[layer, 2], sem_x, (layer, 2), core_peer).wait_send()
        for copy in grad_copies(layer):
            copy.wait_send()
        for k in range(chunks):
            copy_half(layer, k).wait_send()

            def wait(step):
                peer, a_at = ring_peer(step)
                remote(
                    ro.at[layer, a_at, k], ra.at[layer, a, k], sem_ra, (layer, k, step), peer
                ).wait_send()
                remote(
                    ro.at[layer, a, k],
                    grad_weights.at[layer, a, k, :, own_column(layer)],
                    sem_aa,
                    (layer, k, step),
                    peer,
                ).wait_send()

            each_ring(wait)
            for kind in range(7):
                block_copy(layer, k, kind).wait_send()
    for at, eight, around in (
        (0, eight_f.at[0], ring_f.at[0]),
        (1, eight_f.at[1], ring_f.at[1]),
        (2, eight_b.at[1], ring_b.at[1]),
        (3, eight_b.at[0], ring_b.at[0]),
    ):
        for flips in range(1, 8):
            peer, _ = group_peer(flips)
            remote(eight.at[mine], eight.at[mine], sem_e, (at, flips - 1), peer).wait_send()

        def wait_sum(step):
            peer, _ = ring_peer(step)
            remote(around.at[a], around.at[a], sem_r, (at, step), peer).wait_send()

        each_ring(wait_sum)


def body(ring, frames, weights, norm_gain, norm_shift, decays, lengths, cotangent):
    _, views, slots, hidden = frames.shape
    width = round_up(hidden, 4 * LANES)
    rows = views * slots
    padded, chunks, chunk_rows = pick_chunks(hidden, ring)
    dims = (ring, chunks, chunk_rows, views, slots, hidden, width)
    quarter = width // 4
    half = quarter // 2
    vmem = pl.BlockSpec(memory_space=pltpu.VMEM)
    anywhere = pl.BlockSpec(memory_space=pl.ANY)
    scratch = [
        pltpu.VMEM((hidden, hidden), BF16),
        pltpu.VMEM((rows, width), F32),
        pltpu.VMEM((rows, width), F32),
        pltpu.VMEM((rows, width), F32),
        pltpu.VMEM((rows, width), BF16),
        pltpu.VMEM((2, rows, width), F32),
        pltpu.VMEM((2, rows, width), F32),
        pltpu.VMEM((rows, width), F32),
        pltpu.VMEM((2, rows, width), F32),
        pltpu.VMEM((rows, width), BF16),
        pltpu.VMEM((2, 3, rows, width), F32),
        pltpu.VMEM((2, 3, rows, quarter), F32),
        pltpu.VMEM((4 * rows, quarter), BF16),
        pltpu.VMEM((4 * rows, quarter), BF16),
        pltpu.VMEM((2, padded, quarter), F32),
        pltpu.VMEM((2, ring, chunks, chunk_rows, half), F32),
        pltpu.VMEM((2, ring, chunks, chunk_rows, half), F32),
        pltpu.VMEM((8, width), F32),
        pltpu.VMEM((2, width), F32),
        pltpu.VMEM((2, 8, 2, width), F32),
        pltpu.VMEM((2, 8, 4, width), F32),
        pltpu.VMEM((2, ring, 2, width), F32),
        pltpu.VMEM((2, ring, 4, width), F32),
        pltpu.VMEM((2, 2, width), F32),
        pltpu.VMEM((2, 4, width), F32),
        pltpu.SemaphoreType.DMA((3,)),
        pltpu.SemaphoreType.DMA((2, 2, 3)),
        pltpu.SemaphoreType.DMA((2, 2, 3)),
        pltpu.SemaphoreType.DMA((2, 4, 7)),
        pltpu.SemaphoreType.DMA((2, 4, ring)),
        pltpu.SemaphoreType.DMA((2, 2, chunks)),
        pltpu.SemaphoreType.DMA((2, 2, chunks, ring)),
        pltpu.SemaphoreType.DMA((2, 2, chunks, ring)),
        pltpu.SemaphoreType.DMA((2, 2, chunks, 7)),
        pltpu.SemaphoreType.DMA((2, chunks)),
    ]
    small = jax.ShapeDtypeStruct((2, hidden), F32)
    flat = jax.ShapeDtypeStruct((rows, hidden), BF16)
    result, grad_first, grad_weights, grad_gain, grad_shift, grad_decay = pl.pallas_call(
        functools.partial(kernel, dims),
        out_shape=(
            flat,
            flat,
            jax.ShapeDtypeStruct((2, ring, chunks, chunk_rows, width), F32),
            small,
            small,
            small,
        ),
        in_specs=[
            vmem,
            anywhere,
            vmem,
            vmem,
            vmem,
            pl.BlockSpec(memory_space=pltpu.SMEM),
            vmem,
        ],
        out_specs=(vmem, vmem, anywhere, vmem, vmem, vmem),
        scratch_shapes=scratch,
        compiler_params=pltpu.CompilerParams(
            collective_id=0, has_side_effects=True, vmem_limit_bytes=60 << 20
        ),
    )(
        frames.reshape(rows, hidden),
        weights,
        norm_gain,
        norm_shift,
        decays,
        lengths,
        cotangent.reshape(rows, hidden),
    )
    grad_weights = grad_weights.reshape(2, padded, width)[:, :hidden, :hidden]
    return (
        result.reshape(frames.shape),
        grad_first.reshape(frames.shape),
        grad_weights,
        grad_gain,
        grad_shift,
        grad_decay,
    )


def solution(mesh):
    everywhere = P(("dp", "rep"), None, None, None)
    return jax.shard_map(
        functools.partial(body, mesh.shape["dp"] // 2),
        mesh=mesh,
        in_specs=(everywhere, P(), P(), P(), P(), P(("dp", "rep")), everywhere),
        out_specs=(everywhere, everywhere, P(), P(), P(), P()),
        check_vma=False,
    )
```

time: 2050 us -> 423 us (0.21); the launches traced: 2030 us -> 422 us
  waiting for transfers between devices: 1250 us -> 0 us
  local copies, waits for them, and re-layouts: 430 us -> 27.1 us
  Pallas kernels: 0 us -> 394 us
  blocking collectives: 160 us -> 0 us
  other arithmetic: 132 us -> 0 us
  matrix products: 36.9 us -> 0 us
    unnamed x7 -> x0, waiting for transfers between devices: 1060 us -> none
    pallas_call x0 -> x1, Pallas kernels: none -> 394 us  [body(): pl.pallas_call(functools.partial(kernel, dims), out_shape=(flat, flat, ja...]
    slice x111 -> x1, local copies, waits for them, and re-layouts: 231 us -> 23.5 us  [body(): grad_weights = grad_weights.reshape(2, padded, width)[:, :hidden, :hidden]]
    all_gather x1 -> x0, waiting for transfers between devices: 189 us -> none  [body(): gathered = lax.all_gather(summed, 'rep', axis=0, tiled=True)]
    psum x4 -> x0, blocking collectives: 160 us -> none  [the longest x2 80.8 us: back_layer(): lax.psum((jnp.sum(carried * normed, axis=0), jnp.sum(carried, axis=0), jn...]
    unnamed x182 -> x15, local copies, waits for them, and re-layouts: 78.6 us -> 3.6 us
    add x56 -> x0, other arithmetic: 53.7 us -> none  [the longest x30 32.5 us: combine(): return (earlier[0] * latter[0], latter[0] * earlier[1] + latter[1])]
    pad x40 -> x0, local copies, waits for them, and re-layouts: 38.7 us -> none  [recurrence(): lax.associative_scan(combine, (factors, shaped), reverse=reverse, axis=2)]
  transfers between devices with their start and end apart: 4 -> 0, of which waited for: 4 -> 0; matrix products, arithmetic and copies ran while one was open for 0% -> 0% of each run, Pallas kernels for 0% -> 0%
where the time goes in v1:
time: 423 us; the launch traced here: 422 us
  Pallas kernels  394 us (93%)
  local copies, waits for them, and re-layouts  27.1 us (6%)
    pallas_call x1, Pallas kernels, body(): pl.pallas_call(functools.partial(kernel, dims), out_shape=(flat, flat, ja...  394 us
    slice x1, local copies, waits for them, and re-layouts, body(): grad_weights = grad_weights.reshape(2, padded, width)[:, :hidden, :hidden]  23.5 us

profile of v1, /device:TPU:31, one launch (start us, length us, event | category | flops | bytes accessed | tf_op | source)
XLA Modules:
  0.0 422.3 jit_solution(9896670698363169084)
XLA Ops:
  1.3 393.9 %shard_map.118 = (bf16[192,2000]{1,0:T(8,128)(2,1)}, bf16[192,2000]{1,0:T(8,128)(2,1)}, f32[2,4,3,168,2048]{4,3,2,1,0:T(8,128)}, f32[2,2000]{1,0:T(2,128)}, f32[2,2000]{1,0:T(2,128)}, /*index=5*/f32[2,2000]{1,0:T(2,128)}) custom-call(bf16[192,2000]{1,0:T(8,128)(2,1)} %bitcast.6, bf16[2,2000,2000]{2,1,0:T(8,128)(2,1)} %weights.1, f32[2,2000]{1,0:T(2,128)} %gain.1, ...), custom_call_target="tpu_custom_call" | custom-call | tf_op jit(solution)/shard_map/pallas_call | solution.py:736
  395.1 0.0 copy-start.1
  395.2 0.0 copy-start
  395.2 0.0 copy-start.4
  395.2 0.0 copy-start.3
  395.2 0.0 copy-start.2
  395.2 23.5 %slice.4 = f32[2,2000,2000]{2,1,0:T(8,128)} slice(f32[2,2016,2048]{2,1,0:T(8,128)} %bitcast.5), slice={[0:2], [0:2000], [0:2000]} | slice | bytes 64000000 | tf_op jit(solution)/shard_map/slice | solution.py:769
  418.7 0.0 copy-done.1
  418.7 0.9 copy.19
  419.6 0.0 copy-done
  419.6 0.9 copy.20
  420.5 0.0 copy-done.4
  420.5 0.6 copy.21
  421.1 0.0 copy-done.3
  421.1 0.6 copy.22
  421.7 0.0 copy-done.2
  421.7 0.6 copy.23
Async XLA Ops:
  395.1 23.6 %copy-start.1 = (bf16[192,2000]{1,0:T(8,128)(2,1)S(1)}, bf16[192,2000]{1,0:T(8,128)(2,1)}, u32[]{:S(2)}) copy-start(bf16[192,2000]{1,0:T(8,128)(2,1)} %get-tuple-element.12) | copy-start | bytes 2304004
  395.2 24.4 %copy-start = (bf16[192,2000]{1,0:T(8,128)(2,1)S(1)}, bf16[192,2000]{1,0:T(8,128)(2,1)}, u32[]{:S(2)}) copy-start(bf16[192,2000]{1,0:T(8,128)(2,1)} %get-tuple-element.13) | copy-start | bytes 2304004
  395.2 25.3 %copy-start.4 = (f32[2,2000]{1,0:T(2,128)S(1)}, f32[2,2000]{1,0:T(2,128)}, u32[]{:S(2)}) copy-start(f32[2,2000]{1,0:T(2,128)} %get-tuple-element.27) | copy-start | bytes 48004
  395.2 25.9 %copy-start.3 = (f32[2,2000]{1,0:T(2,128)S(1)}, f32[2,2000]{1,0:T(2,128)}, u32[]{:S(2)}) copy-start(f32[2,2000]{1,0:T(2,128)} %get-tuple-element.28) | copy-start | bytes 48004
  395.2 26.5 %copy-start.2 = (f32[2,2000]{1,0:T(2,128)S(1)}, f32[2,2000]{1,0:T(2,128)}, u32[]{:S(2)}) copy-start(f32[2,2000]{1,0:T(2,128)} %get-tuple-element.29) | copy-start | bytes 48004

commit v2 on v1

--- a/solution.py
+++ b/solution.py
@@ -11,6 +11,7 @@
 MESH = pl.DeviceIdType.MESH
 F32 = jnp.float32
 BF16 = jnp.bfloat16
+DELAY = 8
 LANES = 128
 
 
@@ -18,13 +19,13 @@
     return -(-value // unit) * unit
 
 
-def pick_chunks(hidden, ring):
-    best = None
-    for chunks in (3, 4, 2, 1):
-        shard = round_up(-(-hidden // ring), 8 * chunks)
-        if best is None or shard * ring < best[0]:
-            best = (shard * ring, chunks, shard // chunks)
-    return best
+def chunk_plan(hidden, ring, step):
+    plan, start = [], 0
+    while start < hidden:
+        span = min(step, round_up(hidden - start, 8 * ring))
+        plan.append((start, span // ring))
+        start += span
+    return tuple(plan), start
 
 
 def kernel(
@@ -78,11 +79,11 @@
     sem_ag,
     sem_l,
 ):
-    ring, chunks, chunk_rows, views, slots, hidden, width = dims
+    ring, plan, padded, step_rows, views, slots, hidden, width = dims
+    chunks = len(plan)
     rows = views * slots
     quarter = width // 4
     half = quarter // 2
-    padded = ring * chunks * chunk_rows
     blocks = slots // 8
     lane_steps = width // LANES
 
@@ -160,17 +161,27 @@
     diagonal = (device(a, nx, by, nc), device(a, bx, ny, nc))
     sent_x = (x0f, x1r)
 
-    def send_x(layer):
-        to_pair = remote(sent_x[layer], xr.at[layer, 0], sem_x, (layer, 0), pair_peer[layer])
-        to_core = remote(sent_x[layer], xr.at[layer, 1], sem_x, (layer, 1), core_peer)
-        to_pair.start()
-        to_core.start()
-
-    def forward_x(layer):
-        remote(sent_x[layer], xr.at[layer, 0], sem_x, (layer, 0), pair_peer[layer]).wait_recv()
-        remote(xr.at[layer, 0], xr.at[layer, 2], sem_x, (layer, 2), core_peer).start()
-
-    send_x(0)
+    def piece(k):
+        return slice(k * step_rows, (k + 1) * step_rows)
+
+    def x_copy(layer, k, kind):
+        source = sent_x[layer].at[:, piece(k)] if kind < 2 else xr.at[layer, 0, :, piece(k)]
+        return remote(
+            source,
+            xr.at[layer, kind, :, piece(k)],
+            sem_x,
+            (layer, k, kind),
+            core_peer if kind else pair_peer[layer],
+        )
+
+    def send_x(layer, first, last):
+        for k in range(first, last):
+            x_copy(layer, k, 0).start()
+            x_copy(layer, k, 1).start()
+
+    def forward_x(layer, k):
+        x_copy(layer, k, 0).wait_recv()
+        x_copy(layer, k, 2).start()
 
     row_at = lax.broadcasted_iota(jnp.int32, (8, LANES), 0)
     length = lengths[0]
@@ -409,40 +420,51 @@
                 preferred_element_type=F32,
             )
 
-    def wait_factors(layer):
-        remote(sent_x[layer], xr.at[layer, 1], sem_x, (layer, 1), core_peer).wait_recv()
-        remote(xr.at[layer, 0], xr.at[layer, 2], sem_x, (layer, 2), core_peer).wait_recv()
+    def load_factors(layer):
         for copy in grad_copies(layer):
             copy.wait_recv()
-
-    def weight_product(layer):
         gb[0:rows, :] = gpf[layer, :, quarter_at(pair_at[layer], c)].astype(BF16)
         for at in range(3):
             gb[(at + 1) * rows : (at + 2) * rows, :] = gr[layer, at].astype(BF16)
-        for start in range(0, width, quarter):
-            span = min(quarter, padded - start)
-            xchunk[0:rows, :] = sent_x[layer][:, start : start + quarter].astype(BF16)
-            for at in range(3):
-                xchunk[(at + 1) * rows : (at + 2) * rows, :] = xr[
-                    layer, at, :, start : start + quarter
-                ].astype(BF16)
-            product = lax.dot_general(
-                xchunk[...], gb[...], (((0,), (0,)), ((), ())), preferred_element_type=F32
-            )
-            dw[layer, start : start + span, :] = product[:span]
-        if padded > width:
-            dw[layer, width:padded, :] = jnp.zeros((padded - width, quarter), F32)
+
+    def weight_product(layer, k):
+        x_copy(layer, k, 1).wait_recv()
+        x_copy(layer, k, 2).wait_recv()
+        start, shard = plan[k]
+        span = ring * shard
+        xchunk[0:rows, :] = sent_x[layer][:, piece(k)].astype(BF16)
+        for at in range(3):
+            xchunk[(at + 1) * rows : (at + 2) * rows, :] = xr[layer, at, :, piece(k)].astype(BF16)
+        product = lax.dot_general(
+            xchunk[...], gb[...], (((0,), (0,)), ((), ())), preferred_element_type=F32
+        )
+        dw[layer, start : start + span, :] = product[:span]
+
+    def weight_products(layer, first, last):
+        if first == 0:
+            load_factors(layer)
+            forward_x(layer, 0)
+        for k in range(first, last):
+            if k + 1 < chunks:
+                forward_x(layer, k + 1)
+            weight_product(layer, k)
+            copy_half(layer, k).start()
 
     def half_at(o_at):
         return pl.ds(pl.multiple_of(o_at * half, half), half)
 
-    def dw_parts(layer):
-        return dw.at[layer].reshape(ring, chunks, chunk_rows, quarter)
+    def all_rows(k):
+        start, shard = plan[k]
+        return slice(start, start + ring * shard)
+
+    def shard_rows(k, a_at):
+        start, shard = plan[k]
+        return pl.ds(pl.multiple_of(start + a_at * shard, 8), shard)
 
     def copy_half(layer, k):
         return remote(
-            dw_parts(layer).at[:, k, :, half_at(1 - other_at[layer])],
-            ro.at[layer, :, k],
+            dw.at[layer, all_rows(k), half_at(1 - other_at[layer])],
+            ro.at[layer, all_rows(k)],
             sem_ro,
             (layer, k),
             other_peer[layer],
@@ -450,16 +472,14 @@
 
     def reduce_half(layer, k):
         copy_half(layer, k).wait_recv()
-        for at in range(ring):
-            start = (at * chunks + k) * chunk_rows
-            ro[layer, at, k] = (
-                ro[layer, at, k] + dw[layer, start : start + chunk_rows, half_at(other_at[layer])]
-            )
+        ro[layer, all_rows(k)] = (
+            ro[layer, all_rows(k)] + dw[layer, all_rows(k), half_at(other_at[layer])]
+        )
 
         def send(step):
             peer, a_at = ring_peer(step)
             remote(
-                ro.at[layer, a_at, k], ra.at[layer, a, k], sem_ra, (layer, k, step), peer
+                ro.at[layer, shard_rows(k, a_at)], ra.at[layer, shard_rows(k, a)], sem_ra, (layer, k, step), peer
             ).start()
 
         each_ring(send)
@@ -474,8 +494,8 @@
         def wait(step):
             behind = lax.rem(a + ring - step, ring)
             remote(
-                ro.at[layer, a, k],
-                ra.at[layer, behind, k],
+                ro.at[layer, shard_rows(k, a)],
+                ra.at[layer, shard_rows(k, behind)],
                 sem_ra,
                 (layer, k, step),
                 device(behind, bx, by, c),
@@ -484,22 +504,22 @@
         each_ring(wait)
 
         def add(step, total):
-            return total + ra[layer, lax.rem(a + step, ring), k]
-
-        total = ro[layer, a, k]
+            return total + ra[layer, shard_rows(k, lax.rem(a + step, ring))]
+
+        total = ro[layer, shard_rows(k, a)]
         if ring <= 8:
             for step in range(1, ring):
                 total = add(step, total)
         else:
             total = lax.fori_loop(1, ring, add, total)
-        ro[layer, a, k] = total
+        ro[layer, shard_rows(k, a)] = total
         local_copy(layer, k).start()
 
         def send(step):
             peer, _ = ring_peer(step)
             remote(
-                ro.at[layer, a, k],
-                grad_weights.at[layer, a, k, :, own_column(layer)],
+                ro.at[layer, shard_rows(k, a)],
+                grad_weights.at[layer, shard_rows(k, a), own_column(layer)],
                 sem_aa,
                 (layer, k, step),
                 peer,
@@ -509,13 +529,13 @@
 
     def local_copy(layer, k):
         return pltpu.make_async_copy(
-            ro.at[layer, a, k],
-            grad_weights.at[layer, a, k, :, own_column(layer)],
+            ro.at[layer, shard_rows(k, a)],
+            grad_weights.at[layer, shard_rows(k, a), own_column(layer)],
             sem_l.at[layer, k],
         )
 
     def gathered(layer, k, p_at, o_at, c_at):
-        return grad_weights.at[layer, :, k, :, column(layer, p_at, o_at, c_at)]
+        return grad_weights.at[layer, all_rows(k), column(layer, p_at, o_at, c_at)]
 
     def order_of(layer, k):
         pair_first = (k + layer) % 2 == 1
@@ -551,8 +571,8 @@
         def wait(step):
             behind = lax.rem(a + ring - step, ring)
             remote(
-                ro.at[layer, a, k],
-                grad_weights.at[layer, behind, k, :, own_column(layer)],
+                ro.at[layer, shard_rows(k, a)],
+                grad_weights.at[layer, shard_rows(k, behind), own_column(layer)],
                 sem_aa,
                 (layer, k, step),
                 device(behind, bx, by, c),
@@ -575,12 +595,17 @@
         arrived(layer, k, 2)
         block_copy(layer, k, 6).start()
 
+    def shares(at, count):
+        return chunks * at // 8, chunks * count // 8
+
+    send_x(0, *shares(0, 1))
     xb[...] = x0f[...].astype(BF16)
     load_weight(0, 0).wait()
     project(0, xb)
     load_weight(1, 1).start()
     moments(0)
     start_sum(eight_f.at[0], 0)
+    send_x(0, *shares(1, 4))
     gy[:, pl.ds(hidden - hidden % LANES, width - hidden + hidden % LANES)] = jnp.zeros(
         (rows, width - hidden + hidden % LANES), F32
     )
@@ -588,17 +613,21 @@
     middle_sum(eight_f.at[0], ring_f.at[0], 0)
     finish_sum(eight_f.at[0], ring_f.at[0], 0, total_f.at[0])
     forward(0)
-    send_x(1)
+    send_x(1, *shares(0, 1))
     xb[...] = x1r[...].astype(BF16)
     load_weight(1, 1).wait()
     project(1, xb)
     moments(1)
     start_sum(eight_f.at[1], 1)
+    send_x(1, *shares(1, 4))
+    send_x(0, *shares(4, 6))
     middle_sum(eight_f.at[1], ring_f.at[1], 1)
     finish_sum(eight_f.at[1], ring_f.at[1], 1, total_f.at[1])
     forward(1)
     backward_sums(1)
     start_sum(eight_b.at[1], 2)
+    send_x(1, *shares(4, 6))
+    send_x(0, *shares(6, 8))
     output[...] = x1[:, :hidden].astype(BF16)
     middle_sum(eight_b.at[1], ring_b.at[1], 2)
     finish_sum(eight_b.at[1], ring_b.at[1], 2, total_b.at[1])
@@ -609,32 +638,28 @@
     load_weight(0, 2).start()
     backward_sums(0)
     start_sum(eight_b.at[0], 3)
-    forward_x(0)
+    send_x(1, *shares(6, 8))
+    weight_products(1, *shares(0, 3))
     middle_sum(eight_b.at[0], ring_b.at[0], 3)
     finish_sum(eight_b.at[0], ring_b.at[0], 3, total_b.at[0])
     backward_drive(0)
     for copy in grad_copies(0):
         copy.start()
-    forward_x(1)
-    wait_factors(1)
-    weight_product(1)
-    for k in range(chunks):
-        copy_half(1, k).start()
+    weight_products(1, *shares(3, 8))
     load_weight(0, 2).wait()
     back_project()
     grad_frames[...] = gy[:, :hidden].astype(BF16)
-    wait_factors(0)
-    weight_product(0)
-    for k in range(chunks):
-        copy_half(0, k).start()
 
     stages = (reduce_half, reduce_ring, gather_ring, gather_first, gather_second)
+    lag = (0, 2, 4, 6, 9)
     tasks = []
     for layer in (1, 0):
         for k in range(chunks):
             for at, stage in enumerate(stages):
-                tasks.append(((1 - layer) * chunks + k + at, at, layer, k, stage))
-    tasks.sort(key=lambda task: (task[0], -task[1]))
+                due = 2 * k + lag[at] + (0 if layer else DELAY)
+                tasks.append((due, -at, layer, k, stage))
+    tasks.append((DELAY - 2, -9, 0, 0, lambda layer, k: weight_products(0, 0, chunks)))
+    tasks.sort(key=lambda task: task[:2])
     for _, _, layer, k, stage in tasks:
         stage(layer, k)
 
@@ -643,9 +668,9 @@
             for kind in range(3, 7):
                 arrived(layer, k, kind)
     for layer in range(2):
-        remote(sent_x[layer], xr.at[layer, 0], sem_x, (layer, 0), pair_peer[layer]).wait_send()
-        remote(sent_x[layer], xr.at[layer, 1], sem_x, (layer, 1), core_peer).wait_send()
-        remote(xr.at[layer, 0], xr.at[layer, 2], sem_x, (layer, 2), core_peer).wait_send()
+        for k in range(chunks):
+            for kind in range(3):
+                x_copy(layer, k, kind).wait_send()
         for copy in grad_copies(layer):
             copy.wait_send()
         for k in range(chunks):
@@ -654,11 +679,11 @@
             def wait(step):
                 peer, a_at = ring_peer(step)
                 remote(
-                    ro.at[layer, a_at, k], ra.at[layer, a, k], sem_ra, (layer, k, step), peer
+                    ro.at[layer, shard_rows(k, a_at)], ra.at[layer, shard_rows(k, a)], sem_ra, (layer, k, step), peer
                 ).wait_send()
                 remote(
-                    ro.at[layer, a, k],
-                    grad_weights.at[layer, a, k, :, own_column(layer)],
+                    ro.at[layer, shard_rows(k, a)],
+                    grad_weights.at[layer, shard_rows(k, a), own_column(layer)],
                     sem_aa,
                     (layer, k, step),
                     peer,
@@ -688,9 +713,11 @@
     _, views, slots, hidden = frames.shape
     width = round_up(hidden, 4 * LANES)
     rows = views * slots
-    padded, chunks, chunk_rows = pick_chunks(hidden, ring)
-    dims = (ring, chunks, chunk_rows, views, slots, hidden, width)
     quarter = width // 4
+    step_rows = width // 8
+    plan, padded = chunk_plan(hidden, ring, step_rows)
+    chunks = len(plan)
+    dims = (ring, plan, padded, step_rows, views, slots, hidden, width)
     half = quarter // 2
     vmem = pl.BlockSpec(memory_space=pltpu.VMEM)
     anywhere = pl.BlockSpec(memory_space=pl.ANY)
@@ -707,11 +734,11 @@
         pltpu.VMEM((rows, width), BF16),
         pltpu.VMEM((2, 3, rows, width), F32),
         pltpu.VMEM((2, 3, rows, quarter), F32),
-        pltpu.VMEM((4 * rows, quarter), BF16),
+        pltpu.VMEM((4 * rows, step_rows), BF16),
         pltpu.VMEM((4 * rows, quarter), BF16),
         pltpu.VMEM((2, padded, quarter), F32),
-        pltpu.VMEM((2, ring, chunks, chunk_rows, half), F32),
-        pltpu.VMEM((2, ring, chunks, chunk_rows, half), F32),
+        pltpu.VMEM((2, padded, half), F32),
+        pltpu.VMEM((2, padded, half), F32),
         pltpu.VMEM((8, width), F32),
         pltpu.VMEM((2, width), F32),
         pltpu.VMEM((2, 8, 2, width), F32),
@@ -721,7 +748,7 @@
         pltpu.VMEM((2, 2, width), F32),
         pltpu.VMEM((2, 4, width), F32),
         pltpu.SemaphoreType.DMA((3,)),
-        pltpu.SemaphoreType.DMA((2, 2, 3)),
+        pltpu.SemaphoreType.DMA((2, 2, chunks, 3)),
         pltpu.SemaphoreType.DMA((2, 2, 3)),
         pltpu.SemaphoreType.DMA((2, 4, 7)),
         pltpu.SemaphoreType.DMA((2, 4, ring)),
@@ -738,7 +765,7 @@
         out_shape=(
             flat,
             flat,
-            jax.ShapeDtypeStruct((2, ring, chunks, chunk_rows, width), F32),
+            jax.ShapeDtypeStruct((2, padded, width), F32),
             small,
             small,
             small,
@@ -766,7 +793,7 @@
         lengths,
         cotangent.reshape(rows, hidden),
     )
-    grad_weights = grad_weights.reshape(2, padded, width)[:, :hidden, :hidden]
+    grad_weights = grad_weights[:, :hidden, :hidden]
     return (
         result.reshape(frames.shape),
         grad_first.reshape(frames.shape),

time: 423 us -> 367 us (0.87)
  Pallas kernels: 394 us -> 335 us
    pallas_call x1, Pallas kernels: 394 us -> 335 us  [body(): pl.pallas_call(functools.partial(kernel, dims), out_shape=(flat, flat, ja...]
where the time goes in v2:
time: 367 us; the launch traced here: 363 us
  Pallas kernels  335 us (91%)
  local copies, waits for them, and re-layouts  27.1 us (7%)
    pallas_call x1, Pallas kernels, body(): pl.pallas_call(functools.partial(kernel, dims), out_shape=(flat, flat, ja...  335 us
    slice x1, local copies, waits for them, and re-layouts, body(): grad_weights = grad_weights[:, :hidden, :hidden]  23.5 us

profile of v2, /device:TPU:31, one launch (start us, length us, event | category | flops | bytes accessed | tf_op | source)
XLA Modules:
  0.0 363.3 jit_solution(827355399029274083)
XLA Ops:
  1.3 334.8 %shard_map.118 = (bf16[192,2000]{1,0:T(8,128)(2,1)}, bf16[192,2000]{1,0:T(8,128)(2,1)}, f32[2,2016,2048]{2,1,0:T(8,128)}, f32[2,2000]{1,0:T(2,128)}, f32[2,2000]{1,0:T(2,128)}, /*index=5*/f32[2,2000]{1,0:T(2,128)}) custom-call(bf16[192,2000]{1,0:T(8,128)(2,1)} %bitcast.4, bf16[2,2000,2000]{2,1,0:T(8,128)(2,1)} %weights.1, f32[2,2000]{1,0:T(2,128)} %gain.1, ...), custom_call_target="tpu_custom_call" | custom-call | tf_op jit(solution)/shard_map/pallas_call | solution.py:763
  336.1 0.0 copy-start.1
  336.1 0.0 copy-start
  336.1 0.0 copy-start.4
  336.2 0.0 copy-start.3
  336.2 0.0 copy-start.2
  336.2 23.5 %slice.3 = f32[2,2000,2000]{2,1,0:T(8,128)} slice(f32[2,2016,2048]{2,1,0:T(8,128)} %get-tuple-element.14), slice={[0:2], [0:2000], [0:2000]} | slice | bytes 64000000 | tf_op jit(solution)/shard_map/slice | solution.py:796
  359.7 0.0 copy-done.1
  359.7 0.9 copy.19
  360.6 0.0 copy-done
  360.6 0.9 copy.20
  361.4 0.0 copy-done.4
  361.4 0.6 copy.21
  362.1 0.0 copy-done.3
  362.1 0.6 copy.22
  362.7 0.0 copy-done.2
  362.7 0.6 copy.23
Async XLA Ops:
  336.1 23.6 %copy-start.1 = (bf16[192,2000]{1,0:T(8,128)(2,1)S(1)}, bf16[192,2000]{1,0:T(8,128)(2,1)}, u32[]{:S(2)}) copy-start(bf16[192,2000]{1,0:T(8,128)(2,1)} %get-tuple-element.12) | copy-start | bytes 2304004
  336.1 24.4 %copy-start = (bf16[192,2000]{1,0:T(8,128)(2,1)S(1)}, bf16[192,2000]{1,0:T(8,128)(2,1)}, u32[]{:S(2)}) copy-start(bf16[192,2000]{1,0:T(8,128)(2,1)} %get-tuple-element.13) | copy-start | bytes 2304004
  336.1 25.3 %copy-start.4 = (f32[2,2000]{1,0:T(2,128)S(1)}, f32[2,2000]{1,0:T(2,128)}, u32[]{:S(2)}) copy-start(f32[2,2000]{1,0:T(2,128)} %get-tuple-element.27) | copy-start | bytes 48004
  336.2 25.9 %copy-start.3 = (f32[2,2000]{1,0:T(2,128)S(1)}, f32[2,2000]{1,0:T(2,128)}, u32[]{:S(2)}) copy-start(f32[2,2000]{1,0:T(2,128)} %get-tuple-element.28) | copy-start | bytes 48004
  336.2 26.5 %copy-start.2 = (f32[2,2000]{1,0:T(2,128)S(1)}, f32[2,2000]{1,0:T(2,128)}, u32[]{:S(2)}) copy-start(f32[2,2000]{1,0:T(2,128)} %get-tuple-element.29) | copy-start | bytes 48004

commit v3 on v2

v3 whole, which is shorter than its diff:
```python
import functools

import jax
import jax.numpy as jnp
from jax import lax
from jax.experimental import pallas as pl
from jax.experimental.pallas import tpu as pltpu
from jax.sharding import PartitionSpec as P

EPS = 1e-05
MESH = pl.DeviceIdType.MESH
F32 = jnp.float32
BF16 = jnp.bfloat16
LAGS = (0.88, 0.75, 1.41, 1.66, 2.89)
EXTRA = (0.61, 1.4, 2.39)
LANES = 128


def round_up(value, unit):
    return -(-value // unit) * unit


def chunk_plan(hidden, ring, step):
    plan, start = [], 0
    while start < hidden:
        span = min(step, round_up(hidden - start, 8 * ring))
        plan.append((start, span))
        start += span
    return tuple(plan), start


def ring_levels(ring):
    inner = min(4, ring)
    levels = [(1, inner, 0)]
    if ring > inner:
        levels.append((inner, ring // inner, inner))
    return tuple(levels)


def kernel(
    dims,
    frames,
    weights,
    gain,
    shift,
    decay,
    lengths,
    cotangent,
    output,
    grad_frames,
    grad_weights,
    grad_gain,
    grad_shift,
    grad_decay,
    wbuf,
    x0f,
    xb,
    ob,
    xs,
    xo,
    ys,
    yo,
    normed,
    states,
    gy,
    gpf,
    gpb,
    gr,
    xchunk,
    gb,
    dw,
    rb,
    params,
    coef,
    eight_f,
    eight_b,
    ring_f,
    ring_b,
    total_f,
    total_b,
    sem_w,
    sem_io,
    sem_x,
    sem_c,
    sem_y,
    sem_g,
    sem_e,
    sem_r,
    sem_rs,
    sem_az,
    sem_ag,
    sem_l,
):
    ring, plan, _, _, views, slots, hidden, width = dims
    chunks = len(plan)
    rows = views * slots
    piece_at = width // 8
    own_width = width // 8
    levels = ring_levels(ring)
    x1 = gpf.at[0]
    bits = ring.bit_length() - 1
    tile = 512
    blocks = slots // 8
    lane_steps = width // LANES

    dp, rep = lax.axis_index("dp"), lax.axis_index("rep")
    a, bx = dp // 2, dp % 2
    by, c = rep // 2, rep % 2
    nx, ny, nc = 1 - bx, 1 - by, 1 - c

    def device(a_at, x_at, y_at, c_at):
        return (a_at * 2 + x_at, y_at * 2 + c_at)

    core_peer = device(a, bx, by, nc)
    x_peer = device(a, nx, by, c)
    y_peer = device(a, bx, ny, c)

    def group_peer(flips):
        fx, fy, fc = flips // 4, flips // 2 % 2, flips % 2
        x_at, y_at, c_at = (nx if fx else bx), (ny if fy else by), (nc if fc else c)
        return device(a, x_at, y_at, c_at), x_at * 4 + y_at * 2 + c_at

    def ring_peer(level, step):
        stride, size, _ = levels[level]
        at = a // stride % size
        to = lax.rem(at + step, size)
        return device(a + (to - at) * stride, bx, by, c), at, to

    def each_ring(level, act):
        for step in range(1, levels[level][1]):
            act(step)

    def remote(src, dst, sems, at, target):
        return pltpu.make_async_remote_copy(
            src_ref=src,
            dst_ref=dst,
            send_sem=sems.at[(0,) + at],
            recv_sem=sems.at[(1,) + at],
            device_id=target,
            device_id_type=MESH,
        )

    barrier = pltpu.get_barrier_semaphore()
    for flips in range(1, 8):
        pl.semaphore_signal(barrier, 1, device_id=group_peer(flips)[0], device_id_type=MESH)
    for level in range(len(levels)):
        each_ring(
            level,
            lambda step: pl.semaphore_signal(
                barrier, 1, device_id=ring_peer(level, step)[0], device_id_type=MESH
            ),
        )

    def load_weight(layer, at):
        return pltpu.make_async_copy(weights.at[layer], wbuf, sem_w.at[at])

    frames_in = pltpu.make_async_copy(frames, xb, sem_io.at[0])
    frames_in.start()
    load_weight(0, 0).start()
    cotangent_in = pltpu.make_async_copy(cotangent, ob, sem_io.at[1])
    cotangent_in.start()

    length = lengths[0]
    tail = hidden - hidden % LANES
    x0f[:, tail:width] = jnp.broadcast_to(length.astype(F32), (rows, width - tail))
    gy[:, tail:width] = jnp.zeros((rows, width - tail), F32)
    frames_in.wait()
    x0f[:, :hidden] = xb[...].astype(F32)
    params[...] = jnp.zeros(params.shape, F32)
    for at, source in enumerate((gain, shift, decay)):
        params[at * 2 : at * 2 + 2, :hidden] = source[...]
    pl.semaphore_wait(barrier, 7 + sum(size - 1 for _, size, _ in levels))

    def piece(k):
        return slice(k * piece_at, (k + 1) * piece_at)

    def x_copy(k, kind):
        if kind == 3:
            source, target = (xs.at[0], y_peer) if k % 2 == 0 else (xs.at[1], x_peer)
            landing = xs.at[2]
        else:
            source = x0f
            landing, target = ((xs.at[0], x_peer), (xs.at[1], y_peer), (xo.at[0], core_peer))[kind]
        return remote(source.at[:, piece(k)], landing.at[:, piece(k)], sem_x, (k, kind), target)

    def send_x(first, last):
        for k in range(first, last):
            for kind in range(3):
                x_copy(k, kind).start()

    def send_diagonal(first, last):
        for k in range(first, last):
            x_copy(k, k % 2).wait_recv()
            x_copy(k, 3).start()

    def core_copy(at):
        return remote(xs.at[at], xo.at[at + 1], sem_c, (at,), core_peer)

    def wait_x(at):
        for k in range(8):
            if at == 2:
                x_copy(k, 3).wait_recv()
            elif k % 2 != at:
                x_copy(k, at).wait_recv()
        core_copy(at).start()

    def y_copy(at):
        return remote(ys.at[at], yo.at[at], sem_y, (at,), core_peer)

    row_at = lax.broadcasted_iota(jnp.int32, (8, LANES), 0)
    def lanes_of(step):
        return pl.ds(pl.multiple_of(step * LANES, LANES), LANES)

    def over_lanes(act):
        def go(step, _):
            act(lanes_of(step), step)
            return 0

        lax.fori_loop(0, lane_steps, go, 0)

    def valid_at(block, limit=None):
        return (row_at + block * 8).astype(F32) < (length.astype(F32) if limit is None else limit)

    def spread(row):
        return jnp.broadcast_to(row, (8, LANES))

    def row_powers(decay_row, reverse):
        one = spread(decay_row)
        two = one * one
        four = two * two
        from_edge = 7 - row_at if reverse else row_at
        ones = jnp.ones((8, LANES), F32)
        power = (
            one
            * jnp.where(from_edge % 2 == 1, one, ones)
            * jnp.where(from_edge // 2 % 2 == 1, two, ones)
            * jnp.where(from_edge // 4 == 1, four, ones)
        )
        zero = jnp.zeros((8, LANES), F32)
        return (
            jnp.where(from_edge >= 1, one, zero),
            jnp.where(from_edge >= 2, two, zero),
            jnp.where(from_edge >= 4, four, zero),
            power,
        )

    def scan_blocks(values, powers, reverse):
        one, two, four, power = powers
        count = len(values)
        order = range(count - 1, -1, -1) if reverse else range(count)
        result = [None] * count
        carry = None
        for at in order:
            value = values[at]
            for amount, factor in ((1, one), (2, two), (4, four)):
                value = value + factor * pltpu.roll(value, 8 - amount if reverse else amount, 0)
            if carry is not None:
                value = value + power * carry
            carry = spread(value[0:1] if reverse else value[7:8])
            result[at] = value
        return result

    def project(source, result):
        for at in range(0, hidden, tile):
            span = min(tile, hidden - at)
            result[:, at : at + span] = jnp.dot(
                source[...], wbuf[:, at : at + span], preferred_element_type=F32
            )
        if tail < hidden:
            kept = result[:, tail:width]
            lane = lax.broadcasted_iota(jnp.int32, kept.shape, 1)
            result[:, tail:width] = jnp.where(lane < hidden - tail, kept, 0.0)

    mine = bx * 4 + by * 2 + c

    def moments(layer):
        frame_count = (views * length).astype(F32)

        def act(lanes, step):
            first = jnp.zeros((8, LANES), F32)
            square = jnp.zeros((8, LANES), F32)
            for view in range(views):
                for block in range(blocks):
                    value = normed[layer, view * slots + block * 8 : view * slots + block * 8 + 8, lanes]
                    value = jnp.where(valid_at(block), value, 0.0)
                    first += value
                    square += value * value
            first = jnp.sum(first, axis=0, keepdims=True)
            lane = lax.broadcasted_iota(jnp.int32, (1, LANES), 1) + step * LANES
            first = jnp.where(lane >= hidden, frame_count, first)
            eight_f[layer, mine, 0:1, lanes] = first
            eight_f[layer, mine, 1:2, lanes] = jnp.sum(square, axis=0, keepdims=True)

        over_lanes(act)

    def start_sum(eight, at):
        for flips in range(1, 8):
            peer, _ = group_peer(flips)
            remote(eight.at[mine], eight.at[mine], sem_e, (at, flips - 1), peer).start()

    def ring_copy(around, at, level, step, slot):
        _, _, first = levels[level]
        peer, _, _ = ring_peer(level, step)
        ref = around.at[first + slot]
        return remote(ref, ref, sem_r, (at, first + step), peer)

    def ring_send(around, at, level, total):
        _, _, first = levels[level]
        _, own, _ = ring_peer(level, 1)
        around[first + own] = total
        each_ring(level, lambda step: ring_copy(around, at, level, step, own).start())

    def middle_sum(eight, around, at):
        for flips in range(1, 8):
            peer, slot = group_peer(flips)
            remote(eight.at[mine], eight.at[slot], sem_e, (at, flips - 1), peer).wait_recv()
        total = eight[0]
        for slot in range(1, 8):
            total = total + eight[slot]
        ring_send(around, at, 0, total)

    def finish_sum(eight, around, at, result):
        for level, (stride, size, first) in enumerate(levels):

            def wait(step):
                behind = lax.rem(a // stride % size + size - step, size)
                ring_copy(around, at, level, step, behind).wait_recv()

            each_ring(level, wait)
            total = around[first]
            for slot in range(1, size):
                total = total + around[first + slot]
            if level + 1 < len(levels):
                ring_send(around, at, level + 1, total)
        result[...] = total

    def statistics(layer, lanes):
        count = jnp.broadcast_to(total_f[layer, 0:1, width - 1 : width], (1, LANES))
        average = total_f[layer, 0:1, lanes] / count
        variance = total_f[layer, 1:2, lanes] / count - average * average
        return average, lax.rsqrt(variance + EPS), count

    def forward(layer):
        def act(lanes, step):
            average, inverse, _ = statistics(layer, lanes)
            coef[layer : layer + 1, lanes] = inverse
            average, inverse = spread(average), spread(inverse)
            gain_row = spread(params[layer : layer + 1, lanes])
            shift_row = spread(params[2 + layer : 3 + layer, lanes])
            powers = row_powers(params[4 + layer : 5 + layer, lanes], False)
            for view in range(views):
                drives = []
                for block in range(blocks):
                    at = view * slots + block * 8
                    value = (normed[layer, at : at + 8, lanes] - average) * inverse
                    normed[layer, at : at + 8, lanes] = value
                    drives.append(gain_row * value + shift_row)
                result = scan_blocks(drives, powers, False)
                for block in range(blocks):
                    at = view * slots + block * 8
                    state = result[block]
                    states[layer, at : at + 8, lanes] = state
                    bump = jnp.where(valid_at(block), softplus(state), 0.0)
                    if layer == 0:
                        following = x0f[at : at + 8, lanes] + bump
                        x1[at : at + 8, lanes] = following
                        ys[0, at : at + 8, lanes] = following.astype(BF16).astype(F32)
                    else:
                        x1[at : at + 8, lanes] = x1[at : at + 8, lanes] + bump

        over_lanes(act)

    def softplus(state):
        return jnp.maximum(state, 0.0) + jnp.log1p(jnp.exp(-jnp.abs(state)))

    def repeat_forward(at):
        xb[...] = xs[at, :, :hidden].astype(BF16)
        project(xb, ys.at[at + 1])
        limit = spread(xs[at, 0:1, width - LANES : width])
        limit = jnp.broadcast_to(limit[:, LANES - 1 :], (8, LANES))

        def act(lanes, step):
            average, inverse, _ = statistics(0, lanes)
            gain_row = spread(params[0:1, lanes] * inverse)
            shift_row = spread(params[2:3, lanes] - average * inverse * params[0:1, lanes])
            powers = row_powers(params[4:5, lanes], False)
            for view in range(views):
                drives = []
                for block in range(blocks):
                    row = view * slots + block * 8
                    drives.append(gain_row * ys[at + 1, row : row + 8, lanes] + shift_row)
                result = scan_blocks(drives, powers, False)
                for block in range(blocks):
                    row = view * slots + block * 8
                    bump = jnp.where(valid_at(block, limit), softplus(result[block]), 0.0)
                    following = xs[at, row : row + 8, lanes] + bump
                    ys[at + 1, row : row + 8, lanes] = following.astype(BF16).astype(F32)

        over_lanes(act)
        y_copy(at + 1).start()

    def backward_sums(layer):
        def act(lanes, step):
            powers = row_powers(params[4 + layer : 5 + layer, lanes], True)
            sums = [jnp.zeros((8, LANES), F32) for _ in range(3)]
            for view in range(views):
                sources = []
                kept = []
                for block in range(blocks):
                    at = view * slots + block * 8
                    state = states[layer, at : at + 8, lanes]
                    kept.append(state)
                    slope = 1.0 / (1.0 + jnp.exp(-state))
                    slope = gy[at : at + 8, lanes] * slope
                    sources.append(jnp.where(valid_at(block), slope, 0.0))
                carried = scan_blocks(sources, powers, True)
                for block in range(blocks):
                    at = view * slots + block * 8
                    value = carried[block]
                    gpf[layer, at : at + 8, lanes] = value
                    shifted = pltpu.roll(kept[block], 1, 0)
                    before = spread(kept[block - 1][7:8]) if block else jnp.zeros((8, LANES), F32)
                    shifted = jnp.where(row_at == 0, before, shifted)
                    sums[0] += value * normed[layer, at : at + 8, lanes]
                    sums[1] += value
                    sums[2] += value * shifted
            for at in range(3):
                eight_b[layer, mine, at : at + 1, lanes] = jnp.sum(sums[at], axis=0, keepdims=True)
            eight_b[layer, mine, 3:4, lanes] = jnp.zeros((1, LANES), F32)

        over_lanes(act)

    def backward_drive(layer):
        grad_gain[layer : layer + 1, :] = total_b[layer, 0:1, :hidden]
        grad_shift[layer : layer + 1, :] = total_b[layer, 1:2, :hidden]
        grad_decay[layer : layer + 1, :] = total_b[layer, 2:3, :hidden]

        def act(lanes, step):
            count = jnp.broadcast_to(total_f[layer, 0:1, width - 1 : width], (1, LANES))
            slope = spread(total_b[layer, 0:1, lanes] / count)
            offset = spread(total_b[layer, 1:2, lanes] / count)
            scale = spread(coef[layer : layer + 1, lanes] * params[layer : layer + 1, lanes])
            for view in range(views):
                for block in range(0, blocks, 2):
                    pair = []
                    for side in range(2):
                        at = view * slots + (block + side) * 8
                        drop = offset + normed[layer, at : at + 8, lanes] * slope
                        drop = jnp.where(valid_at(block + side), drop, 0.0)
                        pair.append(scale * (gpf[layer, at : at + 8, lanes] - drop))
                    at = view * slots + block * 8
                    low = jnp.concatenate(pair, axis=0).astype(BF16)
                    gpb[at : at + 16, lanes] = low
                    gpf[layer, at : at + 16, lanes] = low.astype(F32)

        over_lanes(act)

    def columns_of(slot):
        return pl.ds(pl.multiple_of(slot * own_width, own_width), own_width)

    def place(flips):
        return flips % 2 * 4 + flips // 4 + flips // 2 % 2 * 2

    def grad_copies(layer):
        result = []
        for flips in (7, 6, 5, 4, 3, 2, 1):
            peer, slot = group_peer(flips)
            result.append(
                remote(
                    gpf.at[layer, :, columns_of(slot)],
                    gr.at[layer, place(flips) - 1],
                    sem_g,
                    (layer, flips - 1),
                    peer,
                )
            )
        return result

    def back_project():
        for at in range(0, hidden, tile):
            span = min(tile, hidden - at)
            gy[:, at : at + span] += lax.dot_general(
                gpb[:, :hidden],
                wbuf[at : at + span, :],
                (((1,), (1,)), ((), ())),
                preferred_element_type=F32,
            )

    def load_factors(layer):
        for copy in grad_copies(layer):
            copy.wait_recv()
        gb[0:rows, :] = gpf[layer, :, columns_of(mine)].astype(BF16)
        for at in range(1, 8):
            gb[at * rows : (at + 1) * rows, :] = gr[layer, at - 1].astype(BF16)
        for at in range(4):
            if layer == 1:
                y_copy(at).wait_recv()
            elif at:
                core_copy(at - 1).wait_recv()
            else:
                for k in range(8):
                    x_copy(k, 2).wait_recv()

    def span_of(k):
        start, span = plan[k]
        return slice(start, start + span)

    def weight_product(layer, k):
        if k == 0:
            load_factors(layer)
        start, span = plan[k]
        for at in range(8):
            if layer == 0:
                source = x0f if at == 0 else xs.at[at - 1] if at < 4 else xo.at[at - 4]
            else:
                source = ys.at[at] if at < 4 else yo.at[at - 4]
            xchunk[at * rows : (at + 1) * rows, :span] = source[:, span_of(k)].astype(BF16)
        dw[layer, span_of(k), :] = lax.dot_general(
            xchunk[:, :span], gb[...], (((0,), (0,)), ((), ())), preferred_element_type=F32
        )
        fold_copy(layer, k, 0).start()

    def bit_of(at):
        return a // 2**at % 2

    def bit_peer(at):
        return device(a + (1 - 2 * bit_of(at)) * 2**at, bx, by, c)

    def region(k, count):
        start, span = plan[k]
        first = start
        for at in range(count):
            first = first + bit_of(at) * (span >> (at + 1))
        return first

    def rows_at(first, count):
        return pl.ds(pl.multiple_of(first, 8), count)

    def fold_copy(layer, k, at):
        start, span = plan[k]
        part = span >> (at + 1)
        source = rows_at(region(k, at) + (1 - bit_of(at)) * part, part)
        landing = start + span - (span >> at)
        return remote(
            dw.at[layer, source],
            rb.at[layer, slice(landing, landing + part)],
            sem_rs,
            (layer, k, at),
            bit_peer(at),
        )

    def fold(layer, k, at):
        fold_copy(layer, k, at).wait_recv()
        start, span = plan[k]
        part = span >> (at + 1)
        landing = start + span - (span >> at)
        kept = rows_at(region(k, at + 1), part)
        dw[layer, kept, :] = dw[layer, kept, :] + rb[layer, landing : landing + part, :]
        if at + 1 < bits:
            fold_copy(layer, k, at + 1).start()
        else:
            local_copy(layer, k).start()
            widen_copy(layer, k, at).start()

    def local_copy(layer, k):
        kept = rows_at(region(k, bits), plan[k][1] >> bits)
        return pltpu.make_async_copy(
            dw.at[layer, kept], grad_weights.at[layer, kept, columns_of(mine)], sem_l.at[layer, k]
        )

    def widen_copy(layer, k, at):
        held = rows_at(region(k, at + 1), plan[k][1] >> (at + 1))
        landing = grad_weights.at[layer, held, columns_of(mine)]
        source = dw.at[layer, held] if at + 1 == bits else landing
        return remote(source, landing, sem_az, (layer, k, at), bit_peer(at))

    def widen(layer, k, at):
        part = plan[k][1] >> (at + 1)
        other = rows_at(region(k, at) + (1 - bit_of(at)) * part, part)
        landing = grad_weights.at[layer, other, columns_of(mine)]
        remote(landing, landing, sem_az, (layer, k, at), bit_peer(at)).wait_recv()
        if at + 1 == bits:
            local_copy(layer, k).wait()
        if at:
            widen_copy(layer, k, at - 1).start()
        else:
            for kind in (0, 1, 3):
                block_copy(layer, k, kind).start()

    def order_of(layer, k):
        own, flip_x = (bx, by), (nx, by)
        flip_y, both = (bx, ny), (nx, ny)
        if (k + layer) % 2 == 1:
            return (own, flip_x, flip_y, both), x_peer, y_peer
        return (own, flip_y, flip_x, both), y_peer, x_peer

    def block(layer, k, x_at, y_at, c_at):
        return grad_weights.at[layer, span_of(k), columns_of(x_at * 4 + y_at * 2 + c_at)]

    def block_copy(layer, k, kind):
        spots, first, second = order_of(layer, k)
        spot, peer = {
            0: (0, first),
            1: (0, second),
            2: (1, second),
            3: (0, core_peer),
            4: (1, core_peer),
            5: (2, core_peer),
            6: (3, core_peer),
        }[kind]
        held = block(layer, k, *spots[spot], c)
        return remote(held, held, sem_ag, (layer, k, kind), peer)

    def arrived(layer, k, kind):
        spots, first, second = order_of(layer, k)
        spot = {0: 1, 1: 2, 2: 3, 3: 0, 4: 1, 5: 2, 6: 3}[kind]
        landing = block(layer, k, *spots[spot], nc if kind >= 3 else c)
        remote(landing, landing, sem_ag, (layer, k, kind), core_peer).wait_recv()

    def gather(layer, k, at):
        arrived(layer, k, at)
        if at == 0:
            block_copy(layer, k, 2).start()
        block_copy(layer, k, 4 + at).start()

    def write_out(target, value, at):
        ob[...] = value
        copy = pltpu.make_async_copy(ob, target, sem_io.at[at])
        copy.start()
        return copy

    send_x(0, 1)
    load_weight(0, 0).wait()
    project(xb, normed.at[0])
    load_weight(1, 1).start()
    moments(0)
    start_sum(eight_f.at[0], 0)
    send_x(1, 4)
    cotangent_in.wait()
    gy[:, :hidden] = ob[...].astype(F32)
    middle_sum(eight_f.at[0], ring_f.at[0], 0)
    finish_sum(eight_f.at[0], ring_f.at[0], 0, total_f.at[0])
    forward(0)
    y_copy(0).start()
    xb[...] = ys[0, :, :hidden].astype(BF16)
    load_weight(1, 1).wait()
    project(xb, normed.at[1])
    moments(1)
    start_sum(eight_f.at[1], 1)
    send_x(4, 7)
    middle_sum(eight_f.at[1], ring_f.at[1], 1)
    finish_sum(eight_f.at[1], ring_f.at[1], 1, total_f.at[1])
    forward(1)
    backward_sums(1)
    start_sum(eight_b.at[1], 2)
    send_x(7, 8)
    send_diagonal(0, 2)
    result_out = write_out(output, x1[:, :hidden].astype(BF16), 2)
    middle_sum(eight_b.at[1], ring_b.at[1], 2)
    finish_sum(eight_b.at[1], ring_b.at[1], 2, total_b.at[1])
    backward_drive(1)
    send_diagonal(2, 8)
    for copy in grad_copies(1):
        copy.start()
    back_project()
    load_weight(0, 2).start()
    backward_sums(0)
    start_sum(eight_b.at[0], 3)
    wait_x(0)
    wait_x(1)
    load_weight(0, 2).wait()
    repeat_forward(0)
    repeat_forward(1)
    wait_x(2)
    repeat_forward(2)

    def finish_backward(layer, k):
        finish_sum(eight_b.at[0], ring_b.at[0], 3, total_b.at[0])
        backward_drive(0)
        for copy in grad_copies(0):
            copy.start()

    def finish_input(layer, k):
        back_project()
        result_out.wait()
        write_out(grad_frames, gy[:, :hidden].astype(BF16), 3)

    stages = [(weight_product, 0.0)]
    for at in range(bits):
        stages.append((functools.partial(fold, at=at), LAGS[0] * (at + 1)))
    for at in range(bits):
        stages.append(
            (functools.partial(widen, at=bits - 1 - at), LAGS[0] * bits + LAGS[1] * (at + 1))
        )
    for at in range(3):
        stages.append(
            (functools.partial(gather, at=at), LAGS[0] * bits + LAGS[1] * bits + LAGS[2 + at])
        )
    tasks = [
        (EXTRA[0], 0, 0, 0, lambda layer, k: middle_sum(eight_b.at[0], ring_b.at[0], 3)),
        (EXTRA[1], 0, 0, 0, finish_backward),
        (EXTRA[2], 0, 0, 0, finish_input),
    ]
    for layer in (1, 0):
        for k in range(chunks):
            for at, (stage, lag) in enumerate(stages):
                tasks.append(((1 - layer) * chunks + k + lag, -at, layer, k, stage))
    tasks.sort(key=lambda task: task[:2])
    for _, _, layer, k, stage in tasks:
        stage(layer, k)

    pltpu.make_async_copy(ob, grad_frames, sem_io.at[3]).wait()
    for k in range(8):
        for kind in range(4):
            x_copy(k, kind).wait_send()
    for at in range(3):
        core_copy(at).wait_send()
    for at in range(4):
        y_copy(at).wait_send()
    for layer in (1, 0):
        for copy in grad_copies(layer):
            copy.wait_send()
        for k in range(chunks):
            for at in range(bits):
                fold_copy(layer, k, at).wait_send()
                widen_copy(layer, k, at).wait_send()
            for kind in range(7):
                block_copy(layer, k, kind).wait_send()
            for kind in range(3, 7):
                arrived(layer, k, kind)
    for at, eight, around in (
        (0, eight_f.at[0], ring_f.at[0]),
        (1, eight_f.at[1], ring_f.at[1]),
        (2, eight_b.at[1], ring_b.at[1]),
        (3, eight_b.at[0], ring_b.at[0]),
    ):
        for flips in range(1, 8):
            peer, _ = group_peer(flips)
            remote(eight.at[mine], eight.at[mine], sem_e, (at, flips - 1), peer).wait_send()
        for level in range(len(levels)):
            _, own, _ = ring_peer(level, 1)
            each_ring(level, lambda step: ring_copy(around, at, level, step, own).wait_send())


def body(ring, frames, weights, norm_gain, norm_shift, decays, lengths, cotangent):
    _, views, slots, hidden = frames.shape
    width = round_up(hidden, 4 * LANES)
    rows = views * slots
    step_rows = width // 8
    own_width = width // 8
    plan, padded = chunk_plan(hidden, ring, step_rows)
    chunks = len(plan)
    dims = (ring, plan, padded, step_rows, views, slots, hidden, width)
    bits = ring.bit_length() - 1
    around = sum(size for _, size, _ in ring_levels(ring))
    vmem = pl.BlockSpec(memory_space=pltpu.VMEM)
    anywhere = pl.BlockSpec(memory_space=pl.ANY)
    scratch = [
        pltpu.VMEM((hidden, hidden), BF16),
        pltpu.VMEM((rows, width), F32),
        pltpu.VMEM((rows, hidden), BF16),
        pltpu.VMEM((rows, hidden), BF16),
        pltpu.VMEM((3, rows, width), F32),
        pltpu.VMEM((4, rows, width), F32),
        pltpu.VMEM((4, rows, width), F32),
        pltpu.VMEM((4, rows, width), F32),
        pltpu.VMEM((2, rows, width), F32),
        pltpu.VMEM((2, rows, width), F32),
        pltpu.VMEM((rows, width), F32),
        pltpu.VMEM((2, rows, width), F32),
        pltpu.VMEM((rows, width), BF16),
        pltpu.VMEM((2, 7, rows, own_width), F32),
        pltpu.VMEM((8 * rows, step_rows), BF16),
        pltpu.VMEM((8 * rows, own_width), BF16),
        pltpu.VMEM((2, padded, own_width), F32),
        pltpu.VMEM((2, padded, own_width), F32),
        pltpu.VMEM((8, width), F32),
        pltpu.VMEM((2, width), F32),
        pltpu.VMEM((2, 8, 2, width), F32),
        pltpu.VMEM((2, 8, 4, width), F32),
        pltpu.VMEM((2, around, 2, width), F32),
        pltpu.VMEM((2, around, 4, width), F32),
        pltpu.VMEM((2, 2, width), F32),
        pltpu.VMEM((2, 4, width), F32),
        pltpu.SemaphoreType.DMA((3,)),
        pltpu.SemaphoreType.DMA((4,)),
        pltpu.SemaphoreType.DMA((2, 8, 4)),
        pltpu.SemaphoreType.DMA((2, 3)),
        pltpu.SemaphoreType.DMA((2, 4)),
        pltpu.SemaphoreType.DMA((2, 2, 7)),
        pltpu.SemaphoreType.DMA((2, 4, 7)),
        pltpu.SemaphoreType.DMA((2, 4, around)),
        pltpu.SemaphoreType.DMA((2, 2, chunks, bits)),
        pltpu.SemaphoreType.DMA((2, 2, chunks, bits)),
        pltpu.SemaphoreType.DMA((2, 2, chunks, 7)),
        pltpu.SemaphoreType.DMA((2, chunks)),
    ]
    small = jax.ShapeDtypeStruct((2, hidden), F32)
    flat = jax.ShapeDtypeStruct((rows, hidden), BF16)
    result, grad_first, grad_weights, grad_gain, grad_shift, grad_decay = pl.pallas_call(
        functools.partial(kernel, dims),
        out_shape=(
            flat,
            flat,
            jax.ShapeDtypeStruct((2, padded, width), F32),
            small,
            small,
            small,
        ),
        in_specs=[
            anywhere,
            anywhere,
            vmem,
            vmem,
            vmem,
            pl.BlockSpec(memory_space=pltpu.SMEM),
            anywhere,
        ],
        out_specs=(anywhere, anywhere, anywhere, vmem, vmem, vmem),
        scratch_shapes=scratch,
        compiler_params=pltpu.CompilerParams(
            collective_id=0, has_side_effects=True, vmem_limit_bytes=60 << 20
        ),
    )(
        frames.reshape(rows, hidden),
        weights,
        norm_gain,
        norm_shift,
        decays,
        lengths,
        cotangent.reshape(rows, hidden),
    )
    grad_weights = grad_weights[:, :hidden, :hidden]
    return (
        result.reshape(frames.shape),
        grad_first.reshape(frames.shape),
        grad_weights,
        grad_gain,
        grad_shift,
        grad_decay,
    )


def solution(mesh):
    everywhere = P(("dp", "rep"), None, None, None)
    return jax.shard_map(
        functools.partial(body, mesh.shape["dp"] // 2),
        mesh=mesh,
        in_specs=(everywhere, P(), P(), P(), P(), P(("dp", "rep")), everywhere),
        out_specs=(everywhere, everywhere, P(), P(), P(), P()),
        check_vma=False,
    )
```

time: 367 us -> 283 us (0.77)
  Pallas kernels: 335 us -> 251 us
    pallas_call x1, Pallas kernels: 335 us -> 251 us  [body(): pl.pallas_call(functools.partial(kernel, dims), out_shape=(flat, flat, ja...]
where the time goes in v3:
time: 283 us; the launch traced here: 280 us
  Pallas kernels  251 us (89%)
  local copies, waits for them, and re-layouts  27.1 us (10%)
    pallas_call x1, Pallas kernels, body(): pl.pallas_call(functools.partial(kernel, dims), out_shape=(flat, flat, ja...  251 us
    slice x1, local copies, waits for them, and re-layouts, body(): grad_weights = grad_weights[:, :hidden, :hidden]  23.5 us

profile of v3, /device:TPU:31, one launch (start us, length us, event | category | flops | bytes accessed | tf_op | source)
XLA Modules:
  0.0 279.5 jit_solution(7356045390298457996)
XLA Ops:
  1.3 251.1 %shard_map.118 = (bf16[192,2000]{1,0:T(8,128)(2,1)}, bf16[192,2000]{1,0:T(8,128)(2,1)}, f32[2,2016,2048]{2,1,0:T(8,128)}, f32[2,2000]{1,0:T(2,128)}, f32[2,2000]{1,0:T(2,128)}, /*index=5*/f32[2,2000]{1,0:T(2,128)}) custom-call(bf16[192,2000]{1,0:T(8,128)(2,1)} %bitcast.4, bf16[2,2000,2000]{2,1,0:T(8,128)(2,1)} %weights.1, f32[2,2000]{1,0:T(2,128)} %gain.1, ...), custom_call_target="tpu_custom_call" | custom-call | tf_op jit(solution)/shard_map/pallas_call | solution.py:800
  252.4 0.0 copy-start.1
  252.4 0.0 copy-start
  252.4 0.0 copy-start.4
  252.4 0.0 copy-start.3
  252.4 0.0 copy-start.2
  252.4 23.5 %slice.3 = f32[2,2000,2000]{2,1,0:T(8,128)} slice(f32[2,2016,2048]{2,1,0:T(8,128)} %get-tuple-element.14), slice={[0:2], [0:2000], [0:2000]} | slice | bytes 64000000 | tf_op jit(solution)/shard_map/slice | solution.py:833
  275.9 0.0 copy-done.1
  275.9 0.9 copy.19
  276.8 0.0 copy-done
  276.8 0.9 copy.20
  277.7 0.0 copy-done.4
  277.7 0.6 copy.21
  278.3 0.0 copy-done.3
  278.3 0.6 copy.22
  278.9 0.0 copy-done.2
  278.9 0.6 copy.23
Async XLA Ops:
  252.4 23.6 %copy-start.1 = (bf16[192,2000]{1,0:T(8,128)(2,1)S(1)}, bf16[192,2000]{1,0:T(8,128)(2,1)}, u32[]{:S(2)}) copy-start(bf16[192,2000]{1,0:T(8,128)(2,1)} %get-tuple-element.12) | copy-start | bytes 2304004
  252.4 24.4 %copy-start = (bf16[192,2000]{1,0:T(8,128)(2,1)S(1)}, bf16[192,2000]{1,0:T(8,128)(2,1)}, u32[]{:S(2)}) copy-start(bf16[192,2000]{1,0:T(8,128)(2,1)} %get-tuple-element.13) | copy-start | bytes 2304004
  252.4 25.3 %copy-start.4 = (f32[2,2000]{1,0:T(2,128)S(1)}, f32[2,2000]{1,0:T(2,128)}, u32[]{:S(2)}) copy-start(f32[2,2000]{1,0:T(2,128)} %get-tuple-element.27) | copy-start | bytes 48004
  252.4 25.9 %copy-start.3 = (f32[2,2000]{1,0:T(2,128)S(1)}, f32[2,2000]{1,0:T(2,128)}, u32[]{:S(2)}) copy-start(f32[2,2000]{1,0:T(2,128)} %get-tuple-element.28) | copy-start | bytes 48004
  252.4 26.5 %copy-start.2 = (f32[2,2000]{1,0:T(2,128)S(1)}, f32[2,2000]{1,0:T(2,128)}, u32[]{:S(2)}) copy-start(f32[2,2000]{1,0:T(2,128)} %get-tuple-element.29) | copy-start | bytes 48004

commit v4 on v3

--- a/solution.py
+++ b/solution.py
@@ -11,8 +11,12 @@
 MESH = pl.DeviceIdType.MESH
 F32 = jnp.float32
 BF16 = jnp.bfloat16
-LAGS = (0.88, 0.75, 1.41, 1.66, 2.89)
-EXTRA = (0.61, 1.4, 2.39)
+LAGS = (1.06, 0.71, 1.63, 1.73, 4.42)
+SUM_DUE = 0.43
+DRIVE_DUE = 1.4
+INPUT_DUE = 2.4
+SHARE = 0.72
+STEPS = 16
 LANES = 128
 
 
@@ -91,7 +95,7 @@
     sem_ag,
     sem_l,
 ):
-    ring, plan, _, _, views, slots, hidden, width = dims
+    ring, plan, padded, _, views, slots, hidden, width = dims
     chunks = len(plan)
     rows = views * slots
     piece_at = width // 8
@@ -697,14 +701,19 @@
             (functools.partial(gather, at=at), LAGS[0] * bits + LAGS[1] * bits + LAGS[2 + at])
         )
     tasks = [
-        (EXTRA[0], 0, 0, 0, lambda layer, k: middle_sum(eight_b.at[0], ring_b.at[0], 3)),
-        (EXTRA[1], 0, 0, 0, finish_backward),
-        (EXTRA[2], 0, 0, 0, finish_input),
+        (SUM_DUE, 0, 0, 0, lambda layer, k: middle_sum(eight_b.at[0], ring_b.at[0], 3)),
+        (DRIVE_DUE, 0, 0, 0, finish_backward),
+        (INPUT_DUE, 0, 0, 0, finish_input),
     ]
     for layer in (1, 0):
         for k in range(chunks):
+            start, span = plan[k]
+            size = span / piece_at
             for at, (stage, lag) in enumerate(stages):
-                tasks.append(((1 - layer) * chunks + k + lag, -at, layer, k, stage))
+                due = ((1 - layer) * padded + start) / piece_at
+                tasks.append(
+                    (due + lag * (SHARE + (1 - SHARE) * size), -at, layer, k, stage)
+                )
     tasks.sort(key=lambda task: task[:2])
     for _, _, layer, k, stage in tasks:
         stage(layer, k)
@@ -746,7 +755,7 @@
     _, views, slots, hidden = frames.shape
     width = round_up(hidden, 4 * LANES)
     rows = views * slots
-    step_rows = width // 8
+    step_rows = max(width // STEPS, 8 * ring)
     own_width = width // 8
     plan, padded = chunk_plan(hidden, ring, step_rows)
     chunks = len(plan)

time: 283 us -> 282 us (level)
  no operation moved by 1% of the time
where the time goes in v4:
time: 282 us; the launch traced here: 279 us
  Pallas kernels  251 us (89%)
  local copies, waits for them, and re-layouts  27.1 us (10%)
    pallas_call x1, Pallas kernels, body(): pl.pallas_call(functools.partial(kernel, dims), out_shape=(flat, flat, ja...  251 us
    slice x1, local copies, waits for them, and re-layouts, body(): grad_weights = grad_weights[:, :hidden, :hidden]  23.5 us

profile of v4, /device:TPU:31, one launch (start us, length us, event | category | flops | bytes accessed | tf_op | source)
XLA Modules:
  0.0 279.2 jit_solution(2458557756179588813)
XLA Ops:
  1.3 250.7 %shard_map.118 = (bf16[192,2000]{1,0:T(8,128)(2,1)}, bf16[192,2000]{1,0:T(8,128)(2,1)}, f32[2,2016,2048]{2,1,0:T(8,128)}, f32[2,2000]{1,0:T(2,128)}, f32[2,2000]{1,0:T(2,128)}, /*index=5*/f32[2,2000]{1,0:T(2,128)}) custom-call(bf16[192,2000]{1,0:T(8,128)(2,1)} %bitcast.4, bf16[2,2000,2000]{2,1,0:T(8,128)(2,1)} %weights.1, f32[2,2000]{1,0:T(2,128)} %gain.1, ...), custom_call_target="tpu_custom_call" | custom-call | tf_op jit(solution)/shard_map/pallas_call | solution.py:809
  252.0 0.0 copy-start.1
  252.0 0.0 copy-start
  252.0 0.0 copy-start.4
  252.0 0.0 copy-start.3
  252.1 0.0 copy-start.2
  252.1 23.5 %slice.3 = f32[2,2000,2000]{2,1,0:T(8,128)} slice(f32[2,2016,2048]{2,1,0:T(8,128)} %get-tuple-element.14), slice={[0:2], [0:2000], [0:2000]} | slice | bytes 64000000 | tf_op jit(solution)/shard_map/slice | solution.py:842
  275.6 0.0 copy-done.1
  275.6 0.9 copy.19
  276.4 0.0 copy-done
  276.5 0.9 copy.20
  277.3 0.0 copy-done.4
  277.3 0.6 copy.21
  277.9 0.0 copy-done.3
  277.9 0.6 copy.22
  278.5 0.0 copy-done.2
  278.6 0.6 copy.23
Async XLA Ops:
  252.0 23.6 %copy-start.1 = (bf16[192,2000]{1,0:T(8,128)(2,1)S(1)}, bf16[192,2000]{1,0:T(8,128)(2,1)}, u32[]{:S(2)}) copy-start(bf16[192,2000]{1,0:T(8,128)(2,1)} %get-tuple-element.12) | copy-start | bytes 2304004
  252.0 24.4 %copy-start = (bf16[192,2000]{1,0:T(8,128)(2,1)S(1)}, bf16[192,2000]{1,0:T(8,128)(2,1)}, u32[]{:S(2)}) copy-start(bf16[192,2000]{1,0:T(8,128)(2,1)} %get-tuple-element.13) | copy-start | bytes 2304004
  252.0 25.3 %copy-start.4 = (f32[2,2000]{1,0:T(2,128)S(1)}, f32[2,2000]{1,0:T(2,128)}, u32[]{:S(2)}) copy-start(f32[2,2000]{1,0:T(2,128)} %get-tuple-element.27) | copy-start | bytes 48004
  252.0 25.9 %copy-start.3 = (f32[2,2000]{1,0:T(2,128)S(1)}, f32[2,2000]{1,0:T(2,128)}, u32[]{:S(2)}) copy-start(f32[2,2000]{1,0:T(2,128)} %get-tuple-element.28) | copy-start | bytes 48004
  252.1 26.5 %copy-start.2 = (f32[2,2000]{1,0:T(2,128)S(1)}, f32[2,2000]{1,0:T(2,128)}, u32[]{:S(2)}) copy-start(f32[2,2000]{1,0:T(2,128)} %get-tuple-element.29) | copy-start | bytes 48004

commit v5 on v4

--- a/solution.py
+++ b/solution.py
@@ -749,6 +749,23 @@
         for level in range(len(levels)):
             _, own, _ = ring_peer(level, 1)
             each_ring(level, lambda step: ring_copy(around, at, level, step, own).wait_send())
+
+
+def settle_kernel(source, result):
+    result[...] = source[:, :, : result.shape[2]]
+
+
+def settle(padded, hidden):
+    layers, _, width = padded.shape
+    step = hidden // 2 if hidden % 16 == 0 else hidden
+    return pl.pallas_call(
+        settle_kernel,
+        grid=(layers, hidden // step),
+        in_specs=[pl.BlockSpec((1, step, width), lambda layer, at: (layer, at, 0))],
+        out_specs=pl.BlockSpec((1, step, hidden), lambda layer, at: (layer, at, 0)),
+        out_shape=jax.ShapeDtypeStruct((layers, hidden, hidden), padded.dtype),
+        compiler_params=pltpu.CompilerParams(vmem_limit_bytes=48 << 20),
+    )(padded)
 
 
 def body(ring, frames, weights, norm_gain, norm_shift, decays, lengths, cotangent):
@@ -839,7 +856,7 @@
         lengths,
         cotangent.reshape(rows, hidden),
     )
-    grad_weights = grad_weights[:, :hidden, :hidden]
+    grad_weights = settle(grad_weights, hidden)
     return (
         result.reshape(frames.shape),
         grad_first.reshape(frames.shape),

time: 282 us -> 281 us (level)
  local copies, waits for them, and re-layouts: 27.1 us -> 3.6 us
  Pallas kernels: 251 us -> 273 us
    slice x1 -> x0, local copies, waits for them, and re-layouts: 23.5 us -> none  [body(): grad_weights = grad_weights[:, :hidden, :hidden]]
    pallas_call x0 -> x1, Pallas kernels: none -> 22.2 us  [settle(): pl.pallas_call(settle_kernel, grid=(layers, hidden // step), in_specs=[pl...]
where the time goes in v5:
time: 281 us; the launch traced here: 278 us
  Pallas kernels  273 us (97%)
  local copies, waits for them, and re-layouts  3.6 us (1%)
    pallas_call x1, Pallas kernels, body(): pl.pallas_call(functools.partial(kernel, dims), out_shape=(flat, flat, ja...  251 us
    pallas_call x1, Pallas kernels, settle(): pl.pallas_call(settle_kernel, grid=(layers, hidden // step), in_specs=[pl...  22.2 us

profile of v5, /device:TPU:31, one launch (start us, length us, event | category | flops | bytes accessed | tf_op | source)
XLA Modules:
  0.0 277.9 jit_solution(4388858756992135062)
XLA Ops:
  1.3 250.7 %shard_map.118 = (bf16[192,2000]{1,0:T(8,128)(2,1)}, bf16[192,2000]{1,0:T(8,128)(2,1)}, f32[2,2016,2048]{2,1,0:T(8,128)}, f32[2,2000]{1,0:T(2,128)}, f32[2,2000]{1,0:T(2,128)}, /*index=5*/f32[2,2000]{1,0:T(2,128)}) custom-call(bf16[192,2000]{1,0:T(8,128)(2,1)} %bitcast.4, bf16[2,2000,2000]{2,1,0:T(8,128)(2,1)} %weights.1, f32[2,2000]{1,0:T(2,128)} %gain.1, ...), custom_call_target="tpu_custom_call" | custom-call | tf_op jit(solution)/shard_map/pallas_call | solution.py:826
  252.0 0.0 copy-start.1
  252.0 0.0 copy-start
  252.0 0.0 copy-start.4
  252.0 0.0 copy-start.3
  252.1 0.0 copy-start.2
  252.1 22.2 %shard_map.119 = f32[2,2000,2000]{2,1,0:T(8,128)} custom-call(f32[2,2016,2048]{2,1,0:T(8,128)} %get-tuple-element.14.source), custom_call_target="tpu_custom_call" | custom-call | tf_op jit(solution)/shard_map/pallas_call | solution.py:761
  274.3 0.0 copy-done.1
  274.3 0.9 copy.19
  275.2 0.0 copy-done
  275.2 0.9 copy.20
  276.0 0.0 copy-done.4
  276.0 0.6 copy.21
  276.6 0.0 copy-done.3
  276.6 0.6 copy.22
  277.3 0.0 copy-done.2
  277.3 0.6 copy.23
Async XLA Ops:
  252.0 22.3 %copy-start.1 = (bf16[192,2000]{1,0:T(8,128)(2,1)S(1)}, bf16[192,2000]{1,0:T(8,128)(2,1)}, u32[]{:S(2)}) copy-start(bf16[192,2000]{1,0:T(8,128)(2,1)} %get-tuple-element.12) | copy-start | bytes 2304004
  252.0 23.1 %copy-start = (bf16[192,2000]{1,0:T(8,128)(2,1)S(1)}, bf16[192,2000]{1,0:T(8,128)(2,1)}, u32[]{:S(2)}) copy-start(bf16[192,2000]{1,0:T(8,128)(2,1)} %get-tuple-element.13) | copy-start | bytes 2304004
  252.0 24.0 %copy-start.4 = (f32[2,2000]{1,0:T(2,128)S(1)}, f32[2,2000]{1,0:T(2,128)}, u32[]{:S(2)}) copy-start(f32[2,2000]{1,0:T(2,128)} %get-tuple-element.27) | copy-start | bytes 48004
  252.0 24.6 %copy-start.3 = (f32[2,2000]{1,0:T(2,128)S(1)}, f32[2,2000]{1,0:T(2,128)}, u32[]{:S(2)}) copy-start(f32[2,2000]{1,0:T(2,128)} %get-tuple-element.28) | copy-start | bytes 48004
  252.1 25.2 %copy-start.2 = (f32[2,2000]{1,0:T(2,128)S(1)}, f32[2,2000]{1,0:T(2,128)}, u32[]{:S(2)}) copy-start(f32[2,2000]{1,0:T(2,128)} %get-tuple-element.29) | copy-start | bytes 48004
